TPU v7x, 256 devices: a whole 4x4x8 slice. The times are simulated.
256 devices in a mesh: seq: 128 (over z, y_hi, x, core), user: 2 (over y_lo).
Axes of the slice: x: 4, y: 4 (y_hi: 2, y_lo: 2; y = y_hi * 2 + y_lo), z: 8, core: 2. Of those that a mesh axis runs over, the one named last changes fastest.
Arguments:
- z_input: bfloat16 [2, 131072, 384], P('user', 'seq'), may hold values from -6 to 6
- gate_input: bfloat16 [2, 131072, 384], P('user', 'seq'), may hold values from -6 to 6
- cotangent: bfloat16 [2, 131072, 384], P('user', 'seq'), may hold values from -6 to 6
- spectrum: bfloat16 [2, 2, 128, 1024, 384], P(None, None, 'seq'), may hold values from -6 to 6
- skip_gain: float32 [384], replicated, may hold values from 0.5 to 1.5
- lengths: int32 [2], P('user'), may hold values from 32768 to 131072, as said below
Outputs:
- z_grad: bfloat16 [2, 131072, 384], P('user', 'seq')
- spectrum_grad: float32 [2, 2, 128, 1024, 384], P(None, None, 'seq', 'user')
Inputs may be any that keep to these rules, and one draw needn't show every extreme that they name: `lengths`: some user's history has all 131072 events.
All inputs are finite; a program needn't handle non-finite values.
Results may differ from a plain program's by a relative error of at most 0.0049.
Values may be sent and summed in bfloat16 or wider, within the bound.
A program may use at most 128 MiB of HBM per device.

v0:
```python
import math

import jax
import jax.numpy as jnp
from jax import lax
from jax.sharding import PartitionSpec as P


def wave_table(period, left_index, right_index):
    product = left_index[:, None] * right_index[None, :] % period
    angles = product.astype(jnp.float32) * (2.0 * math.pi / period)
    return (jnp.cos(angles), jnp.sin(angles))


def transform(real_part, imag_part, cosines, sines, orient, pattern):
    highest = lax.Precision.HIGHEST
    cos_real = jnp.einsum(pattern, cosines, real_part, precision=highest)
    cos_imag = jnp.einsum(pattern, cosines, imag_part, precision=highest)
    sin_real = jnp.einsum(pattern, sines, real_part, precision=highest)
    sin_imag = jnp.einsum(pattern, sines, imag_part, precision=highest)
    return (cos_real - orient * sin_imag, cos_imag + orient * sin_real)


def rotate(real_part, imag_part, cosines, sines, orient):
    return (
        real_part * cosines - orient * imag_part * sines,
        imag_part * cosines + orient * real_part * sines,
    )


def forward_local(real_part, imag_part):
    leading = real_part.shape[:-2]
    seq_span = real_part.shape[-2]
    channel_count = real_part.shape[-1]
    inner = seq_span // 32
    real_part = real_part.reshape(-1, 32, inner, channel_count)
    imag_part = imag_part.reshape(-1, 32, inner, channel_count)
    outer_index = jnp.arange(32, dtype=jnp.int32)
    inner_index = jnp.arange(inner, dtype=jnp.int32)
    cos_outer, sin_outer = wave_table(32, outer_index, outer_index)
    real_part, imag_part = transform(
        real_part, imag_part, cos_outer, sin_outer, -1.0, "ka,eabc->ekbc"
    )
    cos_twist, sin_twist = wave_table(seq_span, outer_index, inner_index)
    real_part, imag_part = rotate(
        real_part, imag_part, cos_twist[None, :, :, None], sin_twist[None, :, :, None], -1.0
    )
    cos_inner, sin_inner = wave_table(inner, inner_index, inner_index)
    real_part, imag_part = transform(
        real_part, imag_part, cos_inner, sin_inner, -1.0, "kb,eabc->ekac"
    )
    shape_out = leading + (seq_span, channel_count)
    return (real_part.reshape(shape_out), imag_part.reshape(shape_out))


def inverse_local(real_part, imag_part):
    leading = real_part.shape[:-2]
    seq_span = real_part.shape[-2]
    channel_count = real_part.shape[-1]
    inner = seq_span // 32
    real_part = real_part.reshape(-1, inner, 32, channel_count)
    imag_part = imag_part.reshape(-1, inner, 32, channel_count)
    outer_index = jnp.arange(32, dtype=jnp.int32)
    inner_index = jnp.arange(inner, dtype=jnp.int32)
    cos_inner, sin_inner = wave_table(inner, inner_index, inner_index)
    real_part, imag_part = transform(
        real_part, imag_part, cos_inner, sin_inner, 1.0, "sb,ebac->esac"
    )
    cos_twist, sin_twist = wave_table(seq_span, inner_index, outer_index)
    real_part, imag_part = rotate(
        real_part, imag_part, cos_twist[None, :, :, None], sin_twist[None, :, :, None], 1.0
    )
    cos_outer, sin_outer = wave_table(32, outer_index, outer_index)
    real_part, imag_part = transform(
        real_part, imag_part, cos_outer, sin_outer, 1.0, "ka,ebac->ekbc"
    )
    shape_out = leading + (seq_span, channel_count)
    return (real_part.reshape(shape_out), imag_part.reshape(shape_out))


def on_device(z_input, gate_input, cotangent, spectrum, skip_gain, lengths):
    seq_count = lax.axis_size("seq")
    my_index = lax.axis_index("seq")
    seq_span = z_input.shape[1]
    rows_block = seq_span // seq_count
    seq_total = seq_span * seq_count
    length_limit = lengths[0]
    own_times = my_index * seq_span + jnp.arange(seq_span, dtype=jnp.int32)
    alive_rows = (own_times < length_limit)[:, None]
    grad_input = jnp.where(
        alive_rows, cotangent[0].astype(jnp.float32) * gate_input[0].astype(jnp.float32), 0.0
    ).astype(jnp.bfloat16)
    masked_z = jnp.where(alive_rows, z_input[0], jnp.zeros_like(z_input[0]))
    stacked = jnp.stack([masked_z, grad_input])[:, None]
    blocks = lax.all_to_all(stacked, "seq", split_axis=2, concat_axis=1, tiled=True)
    values = blocks.astype(jnp.float32)
    device_index = jnp.arange(seq_count, dtype=jnp.int32)
    block_rows = my_index * rows_block + jnp.arange(rows_block, dtype=jnp.int32)
    time_index = device_index[:, None] * seq_span + block_rows[None, :]
    angles = time_index.astype(jnp.float32) * (math.pi / seq_total)
    half_cos = jnp.cos(angles)[None, :, :, None]
    half_sin = jnp.sin(angles)[None, :, :, None]
    real_part = jnp.stack([values, values * half_cos])
    imag_part = jnp.stack([jnp.zeros_like(values), -values * half_sin])
    cos_blocks, sin_blocks = wave_table(seq_count, device_index, device_index)
    real_part, imag_part = transform(
        real_part, imag_part, cos_blocks, sin_blocks, -1.0, "kp,espbc->eskbc"
    )
    cos_shift, sin_shift = wave_table(seq_total, device_index, block_rows)
    real_part, imag_part = rotate(
        real_part,
        imag_part,
        cos_shift[None, None, :, :, None],
        sin_shift[None, None, :, :, None],
        -1.0,
    )
    spectra = jnp.stack([real_part, imag_part])
    received = lax.all_to_all(spectra, "seq", split_axis=3, concat_axis=4, tiled=True)
    all_real, all_imag = forward_local(received[0, :, :, 0], received[1, :, :, 0])
    z_real, g_real = (all_real[:, 0], all_real[:, 1])
    z_imag, g_imag = (all_imag[:, 0], all_imag[:, 1])
    scale_factor = 1.0 / (2.0 * seq_total)
    cross_real = (z_real * g_real + z_imag * g_imag) * scale_factor
    cross_imag = (z_real * g_imag - z_imag * g_real) * scale_factor
    cross_terms = jnp.stack([cross_real, cross_imag], axis=1)[:, :, None]
    spectrum_grad = lax.psum_scatter(cross_terms, "user", scatter_dimension=3, tiled=True)
    filter_real = spectrum[:, 0, 0].astype(jnp.float32)
    filter_imag = spectrum[:, 1, 0].astype(jnp.float32)
    prod_real = filter_real * g_real + filter_imag * g_imag
    prod_imag = filter_real * g_imag - filter_imag * g_real
    real_part, imag_part = inverse_local(prod_real, prod_imag)
    cos_back, sin_back = wave_table(
        seq_total, jnp.reshape(my_index, (1,)), jnp.arange(seq_span, dtype=jnp.int32)
    )
    real_part, imag_part = rotate(
        real_part, imag_part, cos_back[:, :, None], sin_back[:, :, None], 1.0
    )
    returning = jnp.stack([real_part, imag_part])[:, :, None]
    returned = lax.all_to_all(returning, "seq", split_axis=3, concat_axis=2, tiled=True)
    real_part, imag_part = transform(
        returned[0], returned[1], cos_blocks, sin_blocks, 1.0, "pk,ekbc->epbc"
    )
    conv = (real_part[0] + real_part[1] * half_cos[0] - imag_part[1] * half_sin[0]) * scale_factor
    conv_rows = lax.all_to_all(conv, "seq", split_axis=0, concat_axis=1, tiled=True)
    grad_rows = jnp.where(
        alive_rows[None], skip_gain * grad_input.astype(jnp.float32)[None] + conv_rows, 0.0
    ).astype(jnp.bfloat16)
    return (grad_rows, spectrum_grad)


def solution(mesh):
    return jax.shard_map(
        on_device,
        mesh=mesh,
        in_specs=(
            P("user", "seq", None),
            P("user", "seq", None),
            P("user", "seq", None),
            P(None, None, "seq", None, None),
            P(),
            P("user"),
        ),
        out_specs=(P("user", "seq", None), P(None, None, "seq", "user", None)),
        check_vma=False,
    )
```

profile of v0, /device:TPU:7, one launch (start us, length us, event | category | flops | bytes accessed | tf_op | source)
XLA Modules:
  0.0 821.5 jit_solution(7611475697745887626)
XLA Ops:
  7.8 1.3 broadcast_select_fusion
  9.2 1.6 select_convert_fusion
  10.8 0.9 copy-done.2
  11.9 2.8 copy.67
  14.7 15.7 %all-to-all-start = ((bf16[2,1,1024,384]{3,0,1,2:T(2,128)(2,1)}), bf16[2,1,1024,384]{3,0,1,2:T(2,128)(2,1)S(1)}, u32[]{:S(2)}, u32[]{:S(2)}) async-start(bf16[2,1,1024,384]{3,0,1,2:T(2,128)(2,1)} %copy.67), calls=%async_computation | async-start | bytes 3145728 | tf_op jit(solution)/shard_map/all_to_all | solution.py:95
  30.5 40.3 %all-to-all-done = bf16[2,1,1024,384]{3,0,1,2:T(2,128)(2,1)S(1)} async-done(((bf16[2,1,1024,384]{3,0,1,2:T(2,128)(2,1)}), bf16[2,1,1024,384]{3,0,1,2:T(2,128)(2,1)S(1)}, u32[]{:S(2)}, u32[]{:S(2)}) %all-to-all-start) | async-done | bytes 1572896 | tf_op jit(solution)/shard_map/all_to_all | solution.py:95
  70.9 1.9 bitcast_convert_fusion
  72.7 2.9 copy.70
  75.7 0.2 broadcast_multiply_fusion
  75.9 5.6 fusion.22
  81.5 5.3 fusion.23
  86.8 5.5 multiply_add_fusion.1
  92.4 9.1 %fusion.3 = (f32[1,2,2,128,8,384]{3,5,4,2,1,0:T(8,128)}, f32[1,2,2,128,8,384]{3,5,4,2,1,0:T(8,128)}) fusion(f32[2,2,8,384,128]{4,3,2,1,0:T(8,128)S(1)} %multiply_add_fusion.1, f32[128,8]{0,1:T(8,128)S(1)} %get-tuple-element.29, f32[128,8]{0,1:T(8,128)S(1)} %get-tuple-element.28, f32[2,2,8,384,128]{4,3,2,1,0:T(8,128)S(1)} %fusion.23, ...), kind=kOutput, calls=%fused_computation.13 | convolution fusion | flops 1222344704 | bytes 28323840 | tf_op jit(solution)/shard_map/kp,espbc->eskbc/dot_general | solution.py:20
  101.5 10.6 %pad_maximum_fusion = f32[2,2,2,128,8,384]{3,5,4,2,1,0:T(8,128)} fusion(f32[1,2,2,128,8,384]{3,5,4,2,1,0:T(8,128)} %get-tuple-element.9, f32[1,2,2,128,8,384]{3,5,4,2,1,0:T(8,128)} %get-tuple-element.8), kind=kLoop, calls=%fused_computation | loop fusion | flops 3145728 | bytes 25165824 | tf_op jit(solution)/shard_map/stack | solution.py:117
  112.1 12.8 %copy.72 = f32[2,2,2,128,8,384]{5,4,2,1,0,3:T(8,128)} copy(f32[2,2,2,128,8,384]{3,5,4,2,1,0:T(8,128)} %pad_maximum_fusion) | data formatting | bytes 25165824 | tf_op jit(solution)/shard_map/stack | solution.py:117
  124.9 9.3 %all-to-all-start.1 = ((f32[2,2,2,128,8,384]{5,4,2,1,0,3:T(8,128)}), f32[2,2,2,128,8,384]{5,4,2,1,0,3:T(8,128)}, u32[]{:S(2)}, u32[]{:S(2)}) async-start(f32[2,2,2,128,8,384]{5,4,2,1,0,3:T(8,128)} %copy.72), calls=%async_computation.1 | async-start | bytes 25165824 | tf_op jit(solution)/shard_map/all_to_all | solution.py:118
  134.6 0.3 fusion.249
  134.9 2.1 convert.4
  137.0 2.1 convert.5
  139.3 266.8 %all-to-all-done.1 = f32[2,2,2,128,8,384]{5,4,2,1,0,3:T(8,128)} async-done(((f32[2,2,2,128,8,384]{5,4,2,1,0,3:T(8,128)}), f32[2,2,2,128,8,384]{5,4,2,1,0,3:T(8,128)}, u32[]{:S(2)}, u32[]{:S(2)}) %all-to-all-start.1) | async-done | bytes 12582944 | tf_op jit(solution)/shard_map/all_to_all | solution.py:118
  406.1 8.6 %fusion.247 = (f32[1,2,2,128,8,384]{5,4,2,1,0,3:T(8,128)}, f32[1,2,2,128,8,384]{5,4,2,1,0,3:T(8,128)S(1)}) fusion(f32[2,2,2,128,8,384]{5,4,2,1,0,3:T(8,128)} %all-to-all-done.1), kind=kLoop, calls=%fused_computation.278 | loop fusion | bytes 25165824 | tf_op jit(solution)/shard_map/slice | solution.py:119
  414.7 0.4 copy.119
  415.1 10.1 %fusion.16 = f32[4,32,384,32]{2,3,1,0:T(8,128)S(1)} fusion(f32[4,32,32,384]{3,2,1,0:T(8,128)S(1)} %bitcast.198), kind=kOutput, calls=%fused_computation.34 | convolution fusion | flops 603994112 | bytes 12582912 | tf_op jit(solution)/shard_map/ka,eabc->ekbc/dot_general | solution.py:20
  425.2 10.2 %fusion.14 = f32[4,32,384,32]{2,3,1,0:T(8,128)} fusion(f32[4,32,32,384]{3,2,1,0:T(8,128)S(1)} %bitcast.199), kind=kOutput, calls=%fused_computation.32 | convolution fusion | flops 603994112 | bytes 12582912 | tf_op jit(solution)/shard_map/ka,eabc->ekbc/dot_general | solution.py:18
  435.3 0.4 copy.118
  435.8 10.6 %multiply_subtract_fusion = f32[4,32,384,32]{2,3,1,0:T(8,128)} fusion(f32[4,32,384,32]{2,3,1,0:T(8,128)S(1)} %fusion.16, f32[4,32,32,384]{3,2,1,0:T(8,128)S(1)} %bitcast.200), kind=kOutput, calls=%fused_computation.21 | convolution fusion | flops 607139840 | bytes 18874368 | tf_op jit(solution)/shard_map/ka,eabc->ekbc/dot_general | solution.py:17
  446.3 16.4 %fusion = (f32[4,32,32,384]{3,1,2,0:T(8,128)S(1)}, f32[4,32,32,384]{3,1,2,0:T(8,128)S(1)}) fusion(f32[4,32,384,32]{2,3,1,0:T(8,128)} %multiply_subtract_fusion, f32[32,32]{0,1:T(8,128)S(1)} %copy.80, f32[32,32]{0,1:T(8,128)S(1)} %copy.77, f32[4,32,384,32]{2,3,1,0:T(8,128)} %fusion.14, f32[4,32,32,384]{3,2,1,0:T(8,128)S(1)} %bitcast.201), kind=kOutput, calls=%fused_computation.6 | convolution fusion | flops 616577024 | bytes 31465472 | tf_op jit(solution)/shard_map/ka,eabc->ekbc/dot_general | solution.py:19
  462.7 9.9 %fusion.8 = f32[4,32,384,32]{2,3,1,0:T(8,128)S(1)} fusion(f32[4,32,32,384]{3,1,2,0:T(8,128)S(1)} %get-tuple-element.7), kind=kOutput, calls=%fused_computation.26 | convolution fusion | flops 603994112 | bytes 12582912 | tf_op jit(solution)/shard_map/kb,eabc->ekac/dot_general | solution.py:20
  472.6 10.1 %fusion.6 = f32[4,32,384,32]{2,3,1,0:T(8,128)S(1)} fusion(f32[4,32,32,384]{3,1,2,0:T(8,128)S(1)} %get-tuple-element.7), kind=kOutput, calls=%fused_computation.24 | convolution fusion | flops 603994112 | bytes 12582912 | tf_op jit(solution)/shard_map/kb,eabc->ekac/dot_general | solution.py:18
  482.7 10.6 %subtract_bitcast_fusion = f32[4,32,32,384]{3,1,2,0:T(8,128)S(1)} fusion(f32[4,32,384,32]{2,3,1,0:T(8,128)S(1)} %fusion.8, f32[4,32,32,384]{3,1,2,0:T(8,128)S(1)} %get-tuple-element.6), kind=kOutput, calls=%fused_computation.19 | convolution fusion | flops 607139840 | bytes 18874368 | tf_op jit(solution)/shard_map/kb,eabc->ekac/dot_general | solution.py:17
  493.3 3.6 copy.83
  496.9 10.8 %add_bitcast_fusion = f32[4,32,32,384]{3,1,2,0:T(8,128)S(1)} fusion(f32[4,32,384,32]{2,3,1,0:T(8,128)S(1)} %fusion.6, f32[4,32,32,384]{3,1,2,0:T(8,128)S(1)} %get-tuple-element.6), kind=kOutput, calls=%fused_computation.18 | convolution fusion | flops 607139840 | bytes 18874368 | tf_op jit(solution)/shard_map/kb,eabc->ekac/dot_general | solution.py:19
  507.7 3.6 copy.88
  511.4 4.4 add_multiply_fusion
  515.8 10.4 %multiply_add_fusion.3 = (f32[2,32,32,384]{3,1,2,0:T(8,128)S(1)}, f32[2,32,32,384]{3,1,2,0:T(8,128)S(1)}) fusion(f32[2,32,32,384]{3,2,1,0:T(8,128)} %bitcast.207, f32[2,32,32,384]{3,2,1,0:T(8,128)} %convert.5, f32[2,32,32,384]{3,2,1,0:T(8,128)S(1)} %bitcast.206, f32[2,32,32,384]{3,2,1,0:T(8,128)} %convert.4), kind=kLoop, calls=%fused_computation.59 | loop fusion | flops 4718592 | bytes 18874368 | tf_op jit(solution)/shard_map/add | solution.py:129
  526.3 3.0 fusion.99
  529.3 3.2 fusion.97
  532.5 3.2 convolution_subtract_fusion
  535.7 4.1 fusion.24
  539.8 5.3 fusion.28
  545.1 4.9 fusion.26
  550.0 5.1 subtract_bitcast_fusion.2
  555.1 2.0 copy.99
  557.1 4.9 add_bitcast_fusion.2
  562.0 1.8 copy.102
  563.9 0.8 multiply_subtract_fusion.2
  564.6 0.4 maximum_bitcast_fusion
  565.1 7.7 copy.103
  572.7 16.1 %all-to-all-start.2 = ((f32[2,2,1,1024,384]{4,1,0,2,3:T(2,128)}), f32[2,2,1,1024,384]{4,1,0,2,3:T(2,128)}, u32[]{:S(2)}, u32[]{:S(2)}) async-start(f32[2,2,1,1024,384]{4,1,0,2,3:T(2,128)} %copy.103), calls=%async_computation.2 | async-start | bytes 12582912 | tf_op jit(solution)/shard_map/all_to_all | solution.py:139
  588.9 4.9 maximum_bitcast_fusion.1
  593.9 134.8 %all-to-all-done.2 = f32[2,2,1,1024,384]{4,1,0,2,3:T(2,128)} async-done(((f32[2,2,1,1024,384]{4,1,0,2,3:T(2,128)}), f32[2,2,1,1024,384]{4,1,0,2,3:T(2,128)}, u32[]{:S(2)}, u32[]{:S(2)}) %all-to-all-start.2) | async-done | bytes 6291488 | tf_op jit(solution)/shard_map/all_to_all | solution.py:139
  728.7 6.6 fusion.248
  735.3 1.9 copy.172
  737.2 2.4 copy.105
  739.6 3.8 copy.171
  743.4 3.8 copy.107
  747.2 3.0 fusion.64
  750.2 3.0 fusion.62
  753.2 3.0 subtract_bitcast_fusion.1
  756.2 3.0 add_bitcast_fusion.1
  759.2 1.7 fusion.50
  760.9 2.1 copy.110
  763.0 50.0 %all_to_all.19 = f32[128,8,384]{2,1,0:T(8,128)S(1)} all-to-all(f32[128,8,384]{2,1,0:T(8,128)S(1)} %copy.110), channel_id=1, replica_groups=mesh['seq'=128,'user'=2] {'seq'}, dimensions={0} | all-to-all | bytes 3145728 | tf_op jit(solution)/shard_map/all_to_all | solution.py:144
  813.0 1.2 fusion.54
  (43 shorter events, 1.0 us)
Async XLA Ops:
  7.8 1.4 copy-start.9
  10.8 0.9 copy-start.2
  14.7 56.2 %all-to-all-start = ((bf16[2,1,1024,384]{3,0,1,2:T(2,128)(2,1)}), bf16[2,1,1024,384]{3,0,1,2:T(2,128)(2,1)S(1)}, u32[]{:S(2)}, u32[]{:S(2)}) async-start(bf16[2,1,1024,384]{3,0,1,2:T(2,128)(2,1)} %copy.67), calls=%async_computation | async-start | bytes 3145728 | tf_op jit(solution)/shard_map/all_to_all | solution.py:95
  30.5 45.1 %copy-start.7 = (f32[128,8]{0,1:T(8,128)}, f32[128,8]{0,1:T(8,128)S(1)}, u32[]{:S(2)}) copy-start(f32[128,8]{0,1:T(8,128)S(1)} %get-tuple-element.30) | copy-start | bytes 12292
  30.5 61.8 %copy-start.5 = (f32[128,8]{0,1:T(8,128)}, f32[128,8]{0,1:T(8,128)S(1)}, u32[]{:S(2)}) copy-start(f32[128,8]{0,1:T(8,128)S(1)} %get-tuple-element.31) | copy-start | bytes 12292
  124.9 9.7 %copy-start.4 = (bf16[2,2,1,1024,384]{4,3,2,1,0:T(8,128)(2,1)S(1)}, bf16[2,2,1,1024,384]{4,3,2,1,0:T(8,128)(2,1)}, u32[]{:S(2)}) copy-start(bf16[2,2,1,1024,384]{4,3,2,1,0:T(8,128)(2,1)} %param.9) | copy-start | bytes 9437188
  124.9 281.2 %all-to-all-start.1 = ((f32[2,2,2,128,8,384]{5,4,2,1,0,3:T(8,128)}), f32[2,2,2,128,8,384]{5,4,2,1,0,3:T(8,128)}, u32[]{:S(2)}, u32[]{:S(2)}) async-start(f32[2,2,2,128,8,384]{5,4,2,1,0,3:T(8,128)} %copy.72), calls=%async_computation.1 | async-start | bytes 25165824 | tf_op jit(solution)/shard_map/all_to_all | solution.py:118
  415.1 20.3 %slice-start = ((s8[6291456]{0:T(1024)(128)(4,1)}), s8[4194304]{0:T(1024)(128)(4,1)S(1)}, s32[]{:S(2)}) async-start(s8[6291456]{0:T(1024)(128)(4,1)} %bitcast.203), calls=%async_computation.6 | async-start | bytes 8388608
  425.2 10.2 %slice-start.1 = ((s8[6291456]{0:T(1024)(128)(4,1)}), s8[2097152]{0:T(1024)(128)(4,1)S(1)}, s32[]{:S(2)}) async-start(s8[6291456]{0:T(1024)(128)(4,1)} %bitcast.203), calls=%async_computation.7 | async-start | bytes 4194304
  572.7 16.2 %copy-start.1 = (f32[2,1,1024,384]{3,2,1,0:T(8,128)S(1)}, f32[2,1,1024,384]{3,2,1,0:T(8,128)}, u32[]{:S(2)}) copy-start(f32[2,1,1024,384]{3,2,1,0:T(8,128)} %get-tuple-element.10) | copy-start | bytes 9437188
  572.7 155.9 %all-to-all-start.2 = ((f32[2,2,1,1024,384]{4,1,0,2,3:T(2,128)}), f32[2,2,1,1024,384]{4,1,0,2,3:T(2,128)}, u32[]{:S(2)}, u32[]{:S(2)}) async-start(f32[2,2,1,1024,384]{4,1,0,2,3:T(2,128)} %copy.103), calls=%async_computation.2 | async-start | bytes 12582912 | tf_op jit(solution)/shard_map/all_to_all | solution.py:139
  588.9 225.3 %reduce-scatter.2.cloned.1.call-start = ((), (), s32[]{:S(2)}) async-start(), calls=%async_computation.5 | async-start | bytes 9437184 | tf_op jit(solution)/shard_map/reduce_scatter | solution.py:126
  747.2 3.0 copy-start
  756.2 3.0 copy-start.6
  756.2 3.0 copy-start.8
  760.9 52.0 %copy-start.3 = (bf16[1,1024,384]{2,1,0:T(8,128)(2,1)S(1)}, bf16[1,1024,384]{2,1,0:T(8,128)(2,1)}, u32[]{:S(2)}) copy-start(bf16[1,1024,384]{2,1,0:T(8,128)(2,1)} %copy-done.2) | copy-start | bytes 2359300
  760.9 52.0 %copy-start.10 = (pred[1024]{0:T(1024)(128)(4,1)S(1)}, pred[1024]{0:T(1024)(128)(4,1)}, u32[]{:S(2)}) copy-start(pred[1024]{0:T(1024)(128)(4,1)} %copy-done.9) | copy-start | bytes 3076
  760.9 52.0 %copy-start.11 = (f32[384]{0:T(512)S(1)}, f32[384]{0:T(512)}, u32[]{:S(2)}) copy-start(f32[384]{0:T(512)} %param.10) | copy-start | bytes 4612
Sparse Core Ops, SparseCore 0:
  594.0 131.7 reduce-scatter.1
where the time goes:
time: 828 us; the launch traced here: 821 us
  waiting for transfers between devices  442 us (53%)
  matrix products  160 us (19%)
  local copies, waits for them, and re-layouts  68.7 us (8%)
  blocking collectives  50 us (6%)
  other arithmetic  44.4 us (5%)
  starting transfers between devices  41.2 us (5%)
  between operations  15.7 us (2%)
    all_to_all x1, waiting for transfers between devices, on_device(): lax.all_to_all(spectra, 'seq', split_axis=3, concat_axis=4, tiled=True)  267 us
    all_to_all x1, waiting for transfers between devices, on_device(): lax.all_to_all(returning, 'seq', split_axis=3, concat_axis=2, tiled=True)  135 us
    all_to_all x1, blocking collectives, on_device(): lax.all_to_all(conv, 'seq', split_axis=0, concat_axis=1, tiled=True)  50 us
    dot_general x6, matrix products, transform(): sin_real = jnp.einsum(pattern, sines, real_part, precision=highest)  44.7 us
    dot_general x6, matrix products, transform(): sin_imag = jnp.einsum(pattern, sines, imag_part, precision=highest)  40.6 us
    all_to_all x1, waiting for transfers between devices, on_device(): lax.all_to_all(stacked, 'seq', split_axis=2, concat_axis=1, tiled=True)  40.3 us
    dot_general x6, matrix products, transform(): cos_real = jnp.einsum(pattern, cosines, real_part, precision=highest)  37.5 us
    dot_general x6, matrix products, transform(): cos_imag = jnp.einsum(pattern, cosines, imag_part, precision=highest)  36.8 us
  transfers between devices with their start and end apart: 4, of which 3 were waited for; matrix products, arithmetic and copies ran while one was open for 6% of the time, Pallas kernels for 0%

commit v1 on v0

v1 whole, which is shorter than its diff:
```python
import functools

import jax
import jax.numpy as jnp
import ml_dtypes
import numpy as np
from jax import lax
from jax.experimental import pallas as pl
from jax.experimental.pallas import tpu as pltpu
from jax.sharding import PartitionSpec as P

LANES = 128
SUB = 8
PER = 3


def split_bf16(values):
    high = values.astype(ml_dtypes.bfloat16)
    low = (values - high.astype(np.float64)).astype(ml_dtypes.bfloat16)
    return high, low


def tables(n_seq):
    rows = SUB * n_seq
    total = rows * LANES
    index = np.arange(rows)
    freq = (index // SUB) + n_seq * (index % SUB)
    outer, turn = [], []
    for parity in range(2):
        twice = 2 * freq + parity
        angle = (twice[:, None] * index[None, :]) % (2 * rows) * (np.pi / rows)
        outer.append(np.concatenate([np.cos(angle), -np.sin(angle)], 0))
        small = twice[:, None] * np.arange(LANES)[None, :] * (np.pi / total)
        turn.append(np.stack([np.cos(small), -np.sin(small)]))
    outer = np.stack(outer)
    high, low = split_bf16(outer)
    back = np.ascontiguousarray(high.transpose(0, 2, 1))
    lane = np.arange(LANES)
    angle = (lane[:, None] * lane[None, :]) % LANES * (2 * np.pi / LANES)
    cos, sin = np.cos(angle), np.sin(angle)
    forward = np.block([[cos, -sin], [sin, cos]])
    inverse = np.block([[cos, sin], [-sin, cos]])
    fwd_high, fwd_low = split_bf16(forward)
    inv_high, inv_low = split_bf16(inverse)
    inner = np.stack([fwd_high, fwd_low, inv_high, inv_low])
    return high, low, back, np.stack(turn).astype(np.float32), inner


def order(step, n_seq):
    if n_seq % 8:
        return step
    return lax.rem(lax.rem(step, 8) * 3, 8) * (n_seq // 8) + step // 8


def kernel(
    n_seq,
    zg_ref,
    h_ref,
    high_ref,
    low_ref,
    back_ref,
    turn_ref,
    inner_ref,
    s_out,
    c_out,
    zbuf,
    hbuf,
    m_high,
    m_low,
    m_back,
    m_turn,
    m_inner,
    x_buf,
    g_buf,
    b_buf,
    s_send,
    c_part,
    c_other,
    c_send,
    table_sems,
    send_sems,
    recv_sems,
):
    rows = SUB * n_seq
    block = min(256, rows)
    groups = block // SUB
    blocks = rows // block
    scale = 1.0 / (2.0 * rows * LANES)
    seq = lax.axis_index("seq")
    user = lax.axis_index("user")
    core = lax.rem(seq, 2)
    place = seq // 2
    chip = place * 2 + user

    def at_chip(target, which):
        return {"seq": (target // 2) * 2 + which, "user": lax.rem(target, 2)}

    def remote(src, dst, which, device):
        return pltpu.make_async_remote_copy(
            src_ref=src,
            dst_ref=dst,
            send_sem=send_sems.at[which],
            recv_sem=recv_sems.at[which],
            device_id=device,
            device_id_type=pl.DeviceIdType.MESH,
        )

    def scatter(which, src, dst):
        def put(target):
            remote(src.at[target], dst.at[seq], which, at_chip(target, user)).start()

        @pl.when(core == user)
        def _():
            pltpu.make_async_copy(src.at[chip], dst.at[seq], recv_sems.at[which]).start()

        @pl.when(core != user)
        def _():
            put(chip)

        def body(step, carry):
            put(lax.rem(chip + order(step, n_seq), n_seq))
            return carry

        lax.fori_loop(1, n_seq, body, 0)

    def await_all(ref, sem):
        pltpu.make_async_copy(ref, ref, sem).wait()

    def await_sent(which, src):
        @pl.when(core == user)
        def _():
            await_all(src.at[pl.ds(0, n_seq - 1)], send_sems.at[which])

        @pl.when(core != user)
        def _():
            await_all(src, send_sems.at[which])

    scatter(0, zg_ref, zbuf.at[user])
    scatter(1, h_ref, hbuf)

    loads = [
        pltpu.make_async_copy(high_ref.at[core], m_high, table_sems.at[0]),
        pltpu.make_async_copy(low_ref.at[core], m_low, table_sems.at[1]),
        pltpu.make_async_copy(back_ref.at[core], m_back, table_sems.at[2]),
        pltpu.make_async_copy(turn_ref.at[core], m_turn, table_sems.at[3]),
        pltpu.make_async_copy(inner_ref, m_inner, table_sems.at[4]),
    ]
    for load in loads:
        load.start()
    for load in loads:
        load.wait()

    mate = {"seq": seq + 1 - 2 * core, "user": user}
    await_all(zbuf.at[core], recv_sems.at[0])
    swap = remote(zbuf.at[core], zbuf.at[core], 2, mate)
    swap.start()
    swap.wait()

    def forward(channel, carry):
        def fill(part, inner_carry):
            for who in range(2):
                tile = zbuf[who, pl.ds(part * groups, groups), channel]
                tile = tile.astype(jnp.float32)
                at = pl.ds(pl.multiple_of(part * block, block), block)
                for kind in range(2):
                    piece = tile[:, kind * SUB : (kind + 1) * SUB, :]
                    piece = piece.reshape(block, LANES).astype(jnp.bfloat16)
                    left = (2 * who + kind) * LANES
                    x_buf[at, left : left + LANES] = piece
            return inner_carry

        lax.fori_loop(0, blocks, fill, 0)

        def spectrum(part, inner_carry):
            start = pl.multiple_of(part * block, block)
            at = pl.ds(start, block)
            below = pl.ds(pl.multiple_of(rows + part * block, block), block)
            x = x_buf[...]
            dot = functools.partial(jnp.dot, preferred_element_type=jnp.float32)
            y_real = dot(m_high[at, :], x) + dot(m_low[at, :], x)
            y_imag = dot(m_high[below, :], x) + dot(m_low[below, :], x)
            t_real, t_imag = m_turn[0, at, :], m_turn[1, at, :]
            s_real = s_imag = None
            for who in range(2):
                spectra = []
                for kind in range(2):
                    left = (2 * who + kind) * LANES
                    a_real = y_real[:, left : left + LANES]
                    a_imag = y_imag[:, left : left + LANES]
                    mid = jnp.concatenate(
                        [a_real * t_real - a_imag * t_imag, a_real * t_imag + a_imag * t_real],
                        axis=1,
                    ).astype(jnp.bfloat16)
                    spectra.append(dot(mid, m_inner[0]) + dot(mid, m_inner[1]))
                z, g = spectra
                g_buf[channel, who, at, :] = g
                z_real, z_imag = z[:, :LANES], z[:, LANES:]
                g_real, g_imag = g[:, :LANES], g[:, LANES:]
                c_real = z_real * g_real + z_imag * g_imag
                c_imag = z_real * g_imag - z_imag * g_real
                s_real = c_real if who == 0 else s_real + c_real
                s_imag = c_imag if who == 0 else s_imag + c_imag
            s_real, s_imag = s_real * scale, s_imag * scale
            half = LANES // 2
            for who in range(2):
                cut = slice(who * half, (who + 1) * half)
                out = jnp.concatenate([s_real[:, cut], s_imag[:, cut]], axis=1)
                out = out.reshape(groups, SUB, LANES).astype(jnp.bfloat16)
                s_send[pl.ds(who * n_seq + part * groups, groups), channel] = out
            return inner_carry

        lax.fori_loop(0, blocks, spectrum, 0)
        return carry

    lax.fori_loop(0, PER, forward, 0)

    slot = 2 * chip + core

    def put_s(step):
        target = lax.rem(chip + order(step // 2, n_seq), n_seq)
        which = lax.rem(step, 2)
        owner = (target // 2) * 2 + which
        there = lax.rem(target, 2)
        src = s_send.at[there * n_seq + owner]
        remote(src, s_out.at[slot], 3, {"seq": owner, "user": there}).start()

    pltpu.make_async_copy(s_send.at[user * n_seq + seq], s_out.at[slot], recv_sems.at[3]).start()
    put_s(1 - core)

    def body_s(step, carry):
        put_s(step)
        return carry

    lax.fori_loop(2, 2 * n_seq, body_s, 0)

    await_all(hbuf, recv_sems.at[1])

    def inverse(channel, carry):
        dot = functools.partial(jnp.dot, preferred_element_type=jnp.float32)

        def product(part, inner_carry):
            at = pl.ds(pl.multiple_of(part * block, block), block)
            below = pl.ds(pl.multiple_of(rows + part * block, block), block)
            tile = hbuf[pl.ds(part * groups, groups), channel].astype(jnp.float32)
            h_real = tile[:, :SUB, :].reshape(block, LANES)
            h_imag = tile[:, SUB:, :].reshape(block, LANES)
            t_real, t_imag = m_turn[0, at, :], m_turn[1, at, :]
            for who in range(2):
                g = g_buf[channel, who, at, :]
                g_real, g_imag = g[:, :LANES], g[:, LANES:]
                q = jnp.concatenate(
                    [h_real * g_real + h_imag * g_imag, h_real * g_imag - h_imag * g_real],
                    axis=1,
                ).astype(jnp.bfloat16)
                b = dot(q, m_inner[2]) + dot(q, m_inner[3])
                b_real, b_imag = b[:, :LANES], b[:, LANES:]
                left = who * LANES
                b_buf[at, left : left + LANES] = (b_real * t_real + b_imag * t_imag).astype(
                    jnp.bfloat16
                )
                b_buf[below, left : left + LANES] = (b_imag * t_real - b_real * t_imag).astype(
                    jnp.bfloat16
                )
            return inner_carry

        lax.fori_loop(0, blocks, product, 0)

        def fold(part, inner_carry):
            at = pl.ds(pl.multiple_of(part * block, block), block)
            conv = dot(m_back[at, :], b_buf[...]) * scale
            for who in range(2):
                piece = conv[:, who * LANES : (who + 1) * LANES]
                c_part[who, pl.ds(part * groups, groups), channel] = piece.reshape(
                    groups, SUB, LANES
                )
            return inner_carry

        lax.fori_loop(0, blocks, fold, 0)
        return carry

    lax.fori_loop(0, PER, inverse, 0)

    swap_back = remote(c_part.at[1 - core], c_other, 4, mate)
    swap_back.start()
    swap_back.wait()

    def join(part, carry):
        at = pl.ds(part * groups, groups)
        c_send[at] = (c_part[core, at] + c_other[at]).astype(jnp.bfloat16)
        return carry

    lax.fori_loop(0, blocks, join, 0)

    def put_c(target):
        remote(c_send.at[target], c_out.at[chip], 5, {"seq": target, "user": core}).start()

    @pl.when(core == user)
    def _():
        pltpu.make_async_copy(c_send.at[seq], c_out.at[chip], recv_sems.at[5]).start()

    @pl.when(core != user)
    def _():
        put_c(seq)

    def body_c(step, carry):
        put_c(lax.rem(seq + order(step, n_seq), n_seq))
        return carry

    lax.fori_loop(1, n_seq, body_c, 0)

    await_sent(0, zg_ref)
    await_sent(1, h_ref)
    await_all(s_send.at[pl.ds(0, 2 * n_seq - 1)], send_sems.at[3])
    await_sent(5, c_send)
    await_all(s_out, recv_sems.at[3])
    await_all(c_out, recv_sems.at[5])


def mixer(n_seq, zg, h):
    rows = SUB * n_seq
    bf16 = jnp.bfloat16
    high, low, back, turn, inner = (jnp.asarray(t) for t in tables(n_seq))
    anywhere = pl.BlockSpec(memory_space=pl.ANY)
    return pl.pallas_call(
        functools.partial(kernel, n_seq),
        out_shape=(
            jax.ShapeDtypeStruct((2 * n_seq, PER, SUB, LANES), bf16),
            jax.ShapeDtypeStruct((n_seq, PER, SUB, LANES), bf16),
        ),
        in_specs=[anywhere] * 7,
        out_specs=(anywhere, anywhere),
        scratch_shapes=[
            pltpu.VMEM((2, n_seq, PER, 2 * SUB, LANES), bf16),
            pltpu.VMEM((n_seq, PER, 2 * SUB, LANES), bf16),
            pltpu.VMEM((2 * rows, rows), bf16),
            pltpu.VMEM((2 * rows, rows), bf16),
            pltpu.VMEM((rows, 2 * rows), bf16),
            pltpu.VMEM((2, rows, LANES), jnp.float32),
            pltpu.VMEM((4, 2 * LANES, 2 * LANES), bf16),
            pltpu.VMEM((rows, 4 * LANES), bf16),
            pltpu.VMEM((PER, 2, rows, 2 * LANES), jnp.float32),
            pltpu.VMEM((2 * rows, 2 * LANES), bf16),
            pltpu.VMEM((2 * n_seq, PER, SUB, LANES), bf16),
            pltpu.VMEM((2, n_seq, PER, SUB, LANES), jnp.float32),
            pltpu.VMEM((n_seq, PER, SUB, LANES), jnp.float32),
            pltpu.VMEM((n_seq, PER, SUB, LANES), bf16),
            pltpu.SemaphoreType.DMA((5,)),
            pltpu.SemaphoreType.DMA((6,)),
            pltpu.SemaphoreType.DMA((6,)),
        ],
        compiler_params=pltpu.CompilerParams(
            has_side_effects=True, vmem_limit_bytes=58 * 1024 * 1024
        ),
    )(zg, h, high, low, back, turn, inner)


def on_device(z_input, gate_input, cotangent, spectrum, skip_gain, lengths):
    n_seq = lax.axis_size("seq")
    my_seq = lax.axis_index("seq")
    my_user = lax.axis_index("user")
    span, channels = z_input.shape[1:]
    times = my_seq * span + jnp.arange(span, dtype=jnp.int32)
    alive = (times < lengths[0])[:, None]
    grad = jnp.where(
        alive, cotangent[0].astype(jnp.float32) * gate_input[0].astype(jnp.float32), 0.0
    ).astype(jnp.bfloat16)
    masked = jnp.where(alive, z_input[0], jnp.zeros_like(z_input[0]))
    zg = jnp.stack([masked, grad]).reshape(2 * SUB, LANES, channels)
    zg = zg.transpose(2, 0, 1).reshape(n_seq, PER, 2 * SUB, LANES)
    h = lax.dynamic_index_in_dim(spectrum[:, :, 0], my_user, 0, keepdims=False)
    h = h.reshape(2, LANES, SUB, channels).transpose(3, 0, 2, 1)
    h = h.reshape(n_seq, PER, 2 * SUB, LANES)
    s_rows, conv_rows = mixer(n_seq, zg, h)
    s_rows = s_rows.reshape(n_seq, 2, PER, SUB, 2, LANES // 2)
    s_rows = s_rows.transpose(1, 4, 5, 3, 0, 2).astype(jnp.float32)
    spectrum_grad = s_rows.reshape(2, 2, 1, span // 2, channels)
    conv = conv_rows.reshape(channels, span).transpose(1, 0).astype(jnp.float32)
    z_grad = jnp.where(alive, skip_gain * grad.astype(jnp.float32) + conv, 0.0)
    return (z_grad.astype(jnp.bfloat16)[None], spectrum_grad)


def solution(mesh):
    return jax.shard_map(
        on_device,
        mesh=mesh,
        in_specs=(
            P("user", "seq", None),
            P("user", "seq", None),
            P("user", "seq", None),
            P(None, None, "seq", None, None),
            P(),
            P("user"),
        ),
        out_specs=(P("user", "seq", None), P(None, None, "seq", "user", None)),
        check_vma=False,
    )
```

time: 828 us -> 233 us (0.28)
  waiting for transfers between devices: 442 us -> 0 us
  matrix products: 160 us -> 0 us
  Pallas kernels: 0 us -> 141 us
  blocking collectives: 50 us -> 0 us
  starting transfers between devices: 41.2 us -> 0 us
  other arithmetic: 44.4 us -> 5.75 us
  local copies, waits for them, and re-layouts: 68.7 us -> 82.9 us
  between operations: 15.7 us -> 1.53 us
    all_to_all x3 -> x0, waiting for transfers between devices: 442 us -> none  [the longest x1 267 us: on_device(): lax.all_to_all(spectra, 'seq', split_axis=3, concat_axis=4, tiled=True)]
    dot_general x24 -> x0, matrix products: 160 us -> none  [the longest x6 44.7 us: transform(): sin_real = jnp.einsum(pattern, sines, real_part, precision=highest)]
    pallas_call x0 -> x1, Pallas kernels: none -> 141 us  [mixer(): pl.pallas_call(functools.partial(kernel, n_seq), out_shape=(jax.ShapeDtyp...]
    reshape x0 -> x4, local copies, waits for them, and re-layouts: none -> 71.5 us  [the longest x3 68.6 us: on_device(): spectrum_grad = s_rows.reshape(2, 2, 1, span // 2, channels)]
    all_to_all x1 -> x0, blocking collectives: 50 us -> none  [on_device(): lax.all_to_all(conv, 'seq', split_axis=0, concat_axis=1, tiled=True)]
    all_to_all x3 -> x0, starting transfers between devices: 41.2 us -> none  [the longest x1 16.1 us: on_device(): lax.all_to_all(returning, 'seq', split_axis=3, concat_axis=2, tiled=True)]
    slice x3 -> x0, local copies, waits for them, and re-layouts: 15.5 us -> none  [the longest x1 8.55 us: on_device(): received[0, :, :, 0]]
    another operation x1 -> x0, local copies, waits for them, and re-layouts: 12.8 us -> none  [on_device(): spectra = jnp.stack([real_part, imag_part])]
  transfers between devices with their start and end apart: 4 -> 0, of which waited for: 3 -> 0; matrix products, arithmetic and copies ran while one was open for 6% -> 0% of each run, Pallas kernels for 0% -> 0%
where the time goes in v1:
time: 233 us; the launch traced here: 231 us
  Pallas kernels  141 us (61%)
  local copies, waits for them, and re-layouts  82.9 us (36%)
  other arithmetic  5.75 us (2%)
    pallas_call x1, Pallas kernels, mixer(): pl.pallas_call(functools.partial(kernel, n_seq), out_shape=(jax.ShapeDtyp...  141 us
    reshape x3, local copies, waits for them, and re-layouts, on_device(): spectrum_grad = s_rows.reshape(2, 2, 1, span // 2, channels)  68.6 us
    unnamed x14, local copies, waits for them, and re-layouts  6.3 us

profile of v1, /device:TPU:7, one launch (start us, length us, event | category | flops | bytes accessed | tf_op | source)
XLA Modules:
  0.0 230.8 jit_solution(5808849346872712463)
XLA Ops:
  0.6 0.0 copy-start
  0.7 0.0 copy-start.2
  0.7 0.0 copy-start.3
  1.5 1.1 copy-done
  2.5 1.3 broadcast_select_fusion
  3.9 0.0 copy-done.2
  3.9 0.0 copy-done.3
  3.9 0.3 select_convert_fusion
  4.2 1.3 pad_maximum_fusion
  5.5 3.0 %copy.16 = bf16[16,128,384]{1,0,2:T(8,128)(2,1)} copy(bf16[16,128,384]{2,1,0:T(8,128)(2,1)} %bitcast.45) | data formatting | bytes 3145728 | tf_op jit(solution)/shard_map/reshape | solution.py:368
  8.5 1.3 dynamic-slice_bitcast_fusion
  9.8 3.3 %copy.18 = bf16[384,2,8,128]{3,2,1,0:T(8,128)(2,1)} copy(bf16[384,2,8,128]{0,2,3,1:T(8,128)(2,1)} %dynamic-slice_bitcast_fusion) | data formatting | bytes 3145728 | tf_op jit(solution)/shard_map/transpose | solution.py:371
  13.1 140.6 %shard_map.122 = (bf16[256,3,8,128]{3,2,1,0:T(8,128)(2,1)}, bf16[128,3,8,128]{3,2,1,0:T(8,128)(2,1)}) custom-call(bf16[128,3,16,128]{3,2,1,0:T(8,128)(2,1)} %bitcast.47, bf16[128,3,16,128]{3,2,1,0:T(8,128)(2,1)} %bitcast.48, bf16[2,2048,1024]{2,1,0:T(8,128)(2,1)} %constant.31.clone.high_ref, bf16[2,2048,1024]{2,1,0:T(8,128)(2,1)} %constant.32.clone.low_ref, ...), custom_call_target="tpu_custom_call" | custom-call | tf_op jit(solution)/shard_map/pallas_call | solution.py:324
  153.7 1.3 copy.24
  155.0 0.0 copy-start.5
  155.0 0.5 copy.19
  155.5 0.2 copy-done.5
  155.7 0.0 copy-start.4
  155.7 2.8 %fusion.3 = bf16[1,1024,384]{2,1,0:T(8,128)(2,1)} fusion(f32[384,1024]{0,1:T(8,128)S(1)} %copy.19, bf16[1,1024,384]{2,1,0:T(8,128)(2,1)} %param.12, bf16[1,1024,384]{2,1,0:T(8,128)(2,1)} %param.13, f32[384]{0:T(512)S(1)} %copy-done.5, pred[1024]{0:T(1024)(128)(4,1)S(1)} %add_compare_fusion), kind=kLoop, calls=%fused_computation.10 | loop fusion | flops 3932160 | bytes 3934720 | tf_op jit(solution)/shard_map/broadcast_in_dim | solution.py:379
  158.5 0.0 copy-done.4
  158.5 4.9 %reshape.65 = f32[128,2,3,8,2,64]{5,4,3,2,1,0:T(2,128)} reshape(bf16[256,3,8,128]{3,2,1,0:T(8,128)(2,1)S(1)} %copy-done.4) | data formatting | bytes 4718592 | tf_op jit(solution)/shard_map/reshape | solution.py:376
  163.4 27.0 %copy.20 = f32[2,2,64,8,128,3]{3,2,5,4,1,0:T(8,128)} copy(f32[2,2,64,8,128,3]{2,1,3,5,0,4:T(2,128)} %bitcast.44) | data formatting | bytes 6291456 | tf_op jit(solution)/shard_map/reshape | solution.py:376
  190.4 36.7 %reshape.61 = f32[2,2,1,512,384]{3,4,1,0,2:T(8,128)} reshape(f32[2,2,64,8,128,3]{3,2,5,4,1,0:T(8,128)} %copy.20) | data formatting | bytes 6291456 | tf_op jit(solution)/shard_map/reshape | solution.py:376
  227.1 0.0 copy-start.1
  227.1 3.7 %copy.21 = f32[2,2,1,512,384]{4,3,2,1,0:T(8,128)} copy(f32[2,2,1,512,384]{3,4,1,0,2:T(8,128)} %reshape.61) | data formatting | bytes 6291456
  230.8 0.0 copy-done.1
  (1 shorter events, 0.0 us)
Async XLA Ops:
  0.6 1.9 copy-start
  0.7 3.2 %copy-start.2 = (bf16[1,1024,384]{2,1,0:T(8,128)(2,1)S(1)}, bf16[1,1024,384]{2,1,0:T(8,128)(2,1)}, u32[]{:S(2)}) copy-start(bf16[1,1024,384]{2,1,0:T(8,128)(2,1)} %param.12) | copy-start | bytes 2359300
  0.7 3.2 %copy-start.3 = (bf16[1,1024,384]{2,1,0:T(8,128)(2,1)S(1)}, bf16[1,1024,384]{2,1,0:T(8,128)(2,1)}, u32[]{:S(2)}) copy-start(bf16[1,1024,384]{2,1,0:T(8,128)(2,1)} %param.13) | copy-start | bytes 2359300
  155.0 0.7 copy-start.5
  155.7 2.8 %copy-start.4 = (bf16[256,3,8,128]{3,2,1,0:T(8,128)(2,1)S(1)}, bf16[256,3,8,128]{3,2,1,0:T(8,128)(2,1)}, u32[]{:S(2)}) copy-start(bf16[256,3,8,128]{3,2,1,0:T(8,128)(2,1)} %get-tuple-element.5) | copy-start | bytes 4718596
  227.1 3.7 %copy-start.1 = (bf16[2,2,1,1024,384]{4,3,2,1,0:T(8,128)(2,1)S(1)}, bf16[2,2,1,1024,384]{4,3,2,1,0:T(8,128)(2,1)}, u32[]{:S(2)}) copy-start(bf16[2,2,1,1024,384]{4,3,2,1,0:T(8,128)(2,1)} %param.14) | copy-start | bytes 9437188

commit v2 on v1

--- a/solution.py
+++ b/solution.py
@@ -54,15 +54,30 @@
 
 def kernel(
     n_seq,
-    zg_ref,
-    h_ref,
+    z_hbm,
+    gate_hbm,
+    cot_hbm,
+    h_hbm,
+    limit_ref,
     high_ref,
     low_ref,
     back_ref,
     turn_ref,
     inner_ref,
+    s_final,
+    c_final,
+    z_in,
+    gate_in,
+    cot_in,
+    h_in,
+    stage,
+    wide,
+    zg_ref,
+    h_ref,
     s_out,
     c_out,
+    s_turned,
+    c_turned,
     zbuf,
     hbuf,
     m_high,
@@ -77,6 +92,7 @@
     c_part,
     c_other,
     c_send,
+    input_sems,
     table_sems,
     send_sems,
     recv_sems,
@@ -135,9 +151,12 @@
         def _():
             await_all(src, send_sems.at[which])
 
-    scatter(0, zg_ref, zbuf.at[user])
-    scatter(1, h_ref, hbuf)
-
+    inputs = [
+        pltpu.make_async_copy(z_hbm.at[0], z_in, input_sems.at[0]),
+        pltpu.make_async_copy(gate_hbm.at[0], gate_in, input_sems.at[1]),
+        pltpu.make_async_copy(cot_hbm.at[0], cot_in, input_sems.at[2]),
+        pltpu.make_async_copy(h_hbm.at[user, :, 0], h_in, input_sems.at[3]),
+    ]
     loads = [
         pltpu.make_async_copy(high_ref.at[core], m_high, table_sems.at[0]),
         pltpu.make_async_copy(low_ref.at[core], m_low, table_sems.at[1]),
@@ -145,8 +164,60 @@
         pltpu.make_async_copy(turn_ref.at[core], m_turn, table_sems.at[3]),
         pltpu.make_async_copy(inner_ref, m_inner, table_sems.at[4]),
     ]
-    for load in loads:
+    for load in inputs + loads:
         load.start()
+
+    channels = PER * n_seq
+    width = min(LANES, channels)
+    columns = channels // width
+
+    def pack(dst):
+        def body(part, carry):
+            tile = stage[pl.ds(pl.multiple_of(part * 16 * SUB * PER * 2, 8), 16 * SUB * PER * 2), :]
+            dst[pl.ds(part * 16, 16)] = tile.reshape(16, PER, 2 * SUB, LANES).astype(jnp.bfloat16)
+            return carry
+
+        lax.fori_loop(0, n_seq // 16, body, 0)
+
+    for load in inputs[:3]:
+        load.wait()
+
+    def turn_zg(part, carry):
+        at = pl.ds(pl.multiple_of(part * LANES, LANES), LANES)
+        times = seq * (SUB * LANES) + part * LANES
+        times = times + lax.broadcasted_iota(jnp.int32, (LANES, channels), 0)
+        alive = times < limit_ref[0]
+        z = jnp.where(alive, z_in[at, :].astype(jnp.float32), 0.0)
+        g = cot_in[at, :].astype(jnp.float32) * gate_in[at, :].astype(jnp.float32)
+        g = jnp.where(alive, g, 0.0)
+        for column in range(columns):
+            cut = slice(column * width, (column + 1) * width)
+            first = column * width * 2 * SUB + part
+            stage[pl.ds(first, width, stride=2 * SUB), :] = z[:, cut].T
+            stage[pl.ds(first + SUB, width, stride=2 * SUB), :] = g[:, cut].T
+        return carry
+
+    lax.fori_loop(0, SUB, turn_zg, 0)
+    pack(zg_ref)
+    scatter(0, zg_ref, zbuf.at[user])
+
+    inputs[3].wait()
+    for kind in range(2):
+        for column in range(columns):
+            cut = slice(column * width, (column + 1) * width)
+            wide[column, :, :width] = h_in[kind, :, cut].astype(jnp.float32)
+
+        def turn_h(low_bits, carry, kind=kind):
+            for column in range(columns):
+                tile = wide[column, pl.ds(low_bits, LANES, stride=SUB), :]
+                first = column * width * 2 * SUB + kind * SUB + low_bits
+                stage[pl.ds(first, width, stride=2 * SUB), :] = tile.T[:width]
+            return carry
+
+        lax.fori_loop(0, SUB, turn_h, 0)
+    pack(h_ref)
+    scatter(1, h_ref, hbuf)
+
     for load in loads:
         load.wait()
 
@@ -214,7 +285,7 @@
 
     lax.fori_loop(0, PER, forward, 0)
 
-    slot = 2 * chip + core
+    slot = core * n_seq + chip
 
     def put_s(step):
         target = lax.rem(chip + order(step // 2, n_seq), n_seq)
@@ -308,75 +379,124 @@
 
     lax.fori_loop(1, n_seq, body_c, 0)
 
+    def unpack(src):
+        def body(part, carry):
+            tile = src[pl.ds(part * 16, 16)].astype(jnp.float32)
+            size = 16 * PER * SUB
+            stage[pl.ds(pl.multiple_of(part * size, 8), size), :] = tile.reshape(size, LANES)
+            return carry
+
+        lax.fori_loop(0, n_seq // 16, body, 0)
+
+    half = LANES // 2
+    await_all(s_out, recv_sems.at[3])
+    for parity in range(2):
+        unpack(s_out.at[pl.ds(parity * n_seq, n_seq)])
+
+        def turn_s(low_bits, carry):
+            for column in range(columns):
+                first = column * width * SUB + low_bits
+                tile = stage[pl.ds(first, width, stride=SUB), :].T
+                for kind in range(2):
+                    first = kind * half * SUB + low_bits
+                    piece = tile[kind * half : (kind + 1) * half]
+                    wide[column, pl.ds(first, half, stride=SUB), :width] = piece
+            return carry
+
+        lax.fori_loop(0, SUB, turn_s, 0)
+        for column in range(columns):
+            cut = slice(column * width, (column + 1) * width)
+            for kind in range(2):
+                at = pl.ds(kind * half * SUB, half * SUB)
+                s_turned[parity, kind, :, cut] = wide[column, at, :width].astype(jnp.bfloat16)
+    s_store = pltpu.make_async_copy(s_turned, s_final, input_sems.at[0])
+    s_store.start()
+
+    await_all(c_out, recv_sems.at[5])
+    unpack(c_out)
+
+    def turn_c(part, carry):
+        at = pl.ds(pl.multiple_of(part * LANES, LANES), LANES)
+        for column in range(columns):
+            first = column * width * SUB + part
+            tile = stage[pl.ds(first, width, stride=SUB), :].T
+            c_turned[at, column * width : (column + 1) * width] = tile.astype(jnp.bfloat16)
+        return carry
+
+    lax.fori_loop(0, SUB, turn_c, 0)
+    c_store = pltpu.make_async_copy(c_turned, c_final, input_sems.at[1])
+    c_store.start()
+
     await_sent(0, zg_ref)
     await_sent(1, h_ref)
     await_all(s_send.at[pl.ds(0, 2 * n_seq - 1)], send_sems.at[3])
     await_sent(5, c_send)
-    await_all(s_out, recv_sems.at[3])
-    await_all(c_out, recv_sems.at[5])
-
-
-def mixer(n_seq, zg, h):
+    s_store.wait()
+    c_store.wait()
+
+
+def mixer(n_seq, z_input, gate_input, cotangent, spectrum, lengths):
     rows = SUB * n_seq
-    bf16 = jnp.bfloat16
+    span, channels = z_input.shape[1:]
+    bf16, f32 = jnp.bfloat16, jnp.float32
     high, low, back, turn, inner = (jnp.asarray(t) for t in tables(n_seq))
     anywhere = pl.BlockSpec(memory_space=pl.ANY)
     return pl.pallas_call(
         functools.partial(kernel, n_seq),
         out_shape=(
-            jax.ShapeDtypeStruct((2 * n_seq, PER, SUB, LANES), bf16),
-            jax.ShapeDtypeStruct((n_seq, PER, SUB, LANES), bf16),
+            jax.ShapeDtypeStruct((2, 2, span // 2, channels), bf16),
+            jax.ShapeDtypeStruct((span, channels), bf16),
         ),
-        in_specs=[anywhere] * 7,
+        in_specs=[anywhere] * 4 + [pl.BlockSpec(memory_space=pltpu.SMEM)] + [anywhere] * 5,
         out_specs=(anywhere, anywhere),
         scratch_shapes=[
+            pltpu.VMEM((span, channels), bf16),
+            pltpu.VMEM((span, channels), bf16),
+            pltpu.VMEM((span, channels), bf16),
+            pltpu.VMEM((2, span, channels), bf16),
+            pltpu.VMEM((channels * 2 * SUB, LANES), f32),
+            pltpu.VMEM((max(1, channels // LANES), span, LANES), f32),
+            pltpu.VMEM((n_seq, PER, 2 * SUB, LANES), bf16),
+            pltpu.VMEM((n_seq, PER, 2 * SUB, LANES), bf16),
+            pltpu.VMEM((2 * n_seq, PER, SUB, LANES), bf16),
+            pltpu.VMEM((n_seq, PER, SUB, LANES), bf16),
+            pltpu.VMEM((2, 2, span // 2, channels), bf16),
+            pltpu.VMEM((span, channels), bf16),
             pltpu.VMEM((2, n_seq, PER, 2 * SUB, LANES), bf16),
             pltpu.VMEM((n_seq, PER, 2 * SUB, LANES), bf16),
             pltpu.VMEM((2 * rows, rows), bf16),
             pltpu.VMEM((2 * rows, rows), bf16),
             pltpu.VMEM((rows, 2 * rows), bf16),
-            pltpu.VMEM((2, rows, LANES), jnp.float32),
+            pltpu.VMEM((2, rows, LANES), f32),
             pltpu.VMEM((4, 2 * LANES, 2 * LANES), bf16),
             pltpu.VMEM((rows, 4 * LANES), bf16),
-            pltpu.VMEM((PER, 2, rows, 2 * LANES), jnp.float32),
+            pltpu.VMEM((PER, 2, rows, 2 * LANES), f32),
             pltpu.VMEM((2 * rows, 2 * LANES), bf16),
             pltpu.VMEM((2 * n_seq, PER, SUB, LANES), bf16),
-            pltpu.VMEM((2, n_seq, PER, SUB, LANES), jnp.float32),
-            pltpu.VMEM((n_seq, PER, SUB, LANES), jnp.float32),
+            pltpu.VMEM((2, n_seq, PER, SUB, LANES), f32),
+            pltpu.VMEM((n_seq, PER, SUB, LANES), f32),
             pltpu.VMEM((n_seq, PER, SUB, LANES), bf16),
+            pltpu.SemaphoreType.DMA((4,)),
             pltpu.SemaphoreType.DMA((5,)),
             pltpu.SemaphoreType.DMA((6,)),
             pltpu.SemaphoreType.DMA((6,)),
         ],
         compiler_params=pltpu.CompilerParams(
-            has_side_effects=True, vmem_limit_bytes=58 * 1024 * 1024
+            has_side_effects=True, vmem_limit_bytes=60 * 1024 * 1024
         ),
-    )(zg, h, high, low, back, turn, inner)
+    )(z_input, gate_input, cotangent, spectrum, lengths, high, low, back, turn, inner)
 
 
 def on_device(z_input, gate_input, cotangent, spectrum, skip_gain, lengths):
     n_seq = lax.axis_size("seq")
-    my_seq = lax.axis_index("seq")
-    my_user = lax.axis_index("user")
-    span, channels = z_input.shape[1:]
-    times = my_seq * span + jnp.arange(span, dtype=jnp.int32)
+    span = z_input.shape[1]
+    times = lax.axis_index("seq") * span + jnp.arange(span, dtype=jnp.int32)
     alive = (times < lengths[0])[:, None]
-    grad = jnp.where(
-        alive, cotangent[0].astype(jnp.float32) * gate_input[0].astype(jnp.float32), 0.0
-    ).astype(jnp.bfloat16)
-    masked = jnp.where(alive, z_input[0], jnp.zeros_like(z_input[0]))
-    zg = jnp.stack([masked, grad]).reshape(2 * SUB, LANES, channels)
-    zg = zg.transpose(2, 0, 1).reshape(n_seq, PER, 2 * SUB, LANES)
-    h = lax.dynamic_index_in_dim(spectrum[:, :, 0], my_user, 0, keepdims=False)
-    h = h.reshape(2, LANES, SUB, channels).transpose(3, 0, 2, 1)
-    h = h.reshape(n_seq, PER, 2 * SUB, LANES)
-    s_rows, conv_rows = mixer(n_seq, zg, h)
-    s_rows = s_rows.reshape(n_seq, 2, PER, SUB, 2, LANES // 2)
-    s_rows = s_rows.transpose(1, 4, 5, 3, 0, 2).astype(jnp.float32)
-    spectrum_grad = s_rows.reshape(2, 2, 1, span // 2, channels)
-    conv = conv_rows.reshape(channels, span).transpose(1, 0).astype(jnp.float32)
-    z_grad = jnp.where(alive, skip_gain * grad.astype(jnp.float32) + conv, 0.0)
-    return (z_grad.astype(jnp.bfloat16)[None], spectrum_grad)
+    s_rows, conv = mixer(n_seq, z_input, gate_input, cotangent, spectrum, lengths)
+    product = cotangent[0].astype(jnp.float32) * gate_input[0].astype(jnp.float32)
+    grad = product.astype(jnp.bfloat16).astype(jnp.float32)
+    z_grad = jnp.where(alive, skip_gain * grad + conv.astype(jnp.float32), 0.0)
+    return (z_grad.astype(jnp.bfloat16)[None], s_rows.astype(jnp.float32)[:, :, None])
 
 
 def solution(mesh):

time: 233 us -> 152 us (0.65)
  local copies, waits for them, and re-layouts: 82.9 us -> 0.02 us
  Pallas kernels: 141 us -> 146 us
    reshape x4 -> x0, local copies, waits for them, and re-layouts: 71.5 us -> none  [the longest x3 68.6 us: on_device(): spectrum_grad = s_rows.reshape(2, 2, 1, span // 2, channels)]
    unnamed x14 -> x8, local copies, waits for them, and re-layouts: 6.3 us -> 0.02 us
    pallas_call x1, Pallas kernels: 141 us -> 146 us  [mixer(): pl.pallas_call(functools.partial(kernel, n_seq), out_shape=(jax.ShapeDtyp...]
    transpose x2 -> x0, local copies, waits for them, and re-layouts: 4.59 us -> none  [on_device(): h = h.reshape(2, LANES, SUB, channels).transpose(3, 0, 2, 1)]
where the time goes in v2:
time: 152 us
  Pallas kernels  146 us (96%)
  other arithmetic  4.42 us (3%)
    pallas_call x1, Pallas kernels, mixer(): pl.pallas_call(functools.partial(kernel, n_seq), out_shape=(jax.ShapeDtyp...  146 us

profile of v2, /device:TPU:7, one launch (start us, length us, event | category | flops | bytes accessed | tf_op | source)
XLA Modules:
  0.0 152.0 jit_solution(10159638881867763894)
XLA Ops:
  1.3 0.0 copy-start
  1.3 0.0 copy-start.1
  1.3 0.0 copy-start.3
  1.3 146.2 %shard_map.122 = (bf16[2,2,512,384]{3,2,1,0:T(8,128)(2,1)}, bf16[1024,384]{1,0:T(8,128)(2,1)}) custom-call(bf16[1,1024,384]{2,1,0:T(8,128)(2,1)} %z_hbm.1, bf16[1,1024,384]{2,1,0:T(8,128)(2,1)} %gate_hbm.1, bf16[1,1024,384]{2,1,0:T(8,128)(2,1)} %cot_hbm.1, bf16[2,2,1,1024,384]{4,3,2,1,0:T(8,128)(2,1)} %h_hbm.1, s32[1]{0:T(128)} %copy.14.limit_ref, ...), custom_call_target="tpu_custom_call" | custom-call | tf_op jit(solution)/shard_map/pallas_call | solution.py:444
  147.5 0.0 copy-done
  147.5 0.0 copy-done.1
  147.5 0.0 copy-done.3
  147.5 0.0 copy-start.2
  147.6 2.5 %fusion.4 = bf16[1,1024,384]{2,1,0:T(8,128)(2,1)} fusion(bf16[1024,384]{1,0:T(8,128)(2,1)} %get-tuple-element.4, bf16[1,1024,384]{2,1,0:T(8,128)(2,1)S(1)} %copy-done, bf16[1,1024,384]{2,1,0:T(8,128)(2,1)S(1)} %copy-done.1, f32[384]{0:T(512)S(1)} %copy-done.3, pred[1024]{0:T(1024)(128)(4,1)S(1)} %add_compare_fusion), kind=kLoop, calls=%fused_computation.7 | loop fusion | flops 3932160 | bytes 3148288 | tf_op jit(solution)/shard_map/broadcast_in_dim | solution.py:499
  150.1 0.0 copy-done.2
  150.1 1.9 %bitcast_convert_fusion = f32[2,2,1,512,384]{4,3,2,1,0:T(8,128)} fusion(bf16[2,2,512,384]{3,2,1,0:T(8,128)(2,1)S(1)} %copy-done.2), kind=kLoop, calls=%fused_computation | loop fusion | flops 786432 | bytes 4718592
  (1 shorter events, 0.0 us)
Async XLA Ops:
  1.3 146.2 %copy-start = (bf16[1,1024,384]{2,1,0:T(8,128)(2,1)S(1)}, bf16[1,1024,384]{2,1,0:T(8,128)(2,1)}, u32[]{:S(2)}) copy-start(bf16[1,1024,384]{2,1,0:T(8,128)(2,1)} %gate_hbm.1) | copy-start | bytes 2359300
  1.3 146.2 %copy-start.1 = (bf16[1,1024,384]{2,1,0:T(8,128)(2,1)S(1)}, bf16[1,1024,384]{2,1,0:T(8,128)(2,1)}, u32[]{:S(2)}) copy-start(bf16[1,1024,384]{2,1,0:T(8,128)(2,1)} %cot_hbm.1) | copy-start | bytes 2359300
  1.3 146.2 %copy-start.3 = (f32[384]{0:T(512)S(1)}, f32[384]{0:T(512)}, u32[]{:S(2)}) copy-start(f32[384]{0:T(512)} %param.15) | copy-start | bytes 4612
  147.5 2.6 %copy-start.2 = (bf16[2,2,512,384]{3,2,1,0:T(8,128)(2,1)S(1)}, bf16[2,2,512,384]{3,2,1,0:T(8,128)(2,1)}, u32[]{:S(2)}) copy-start(bf16[2,2,512,384]{3,2,1,0:T(8,128)(2,1)} %get-tuple-element.5) | copy-start | bytes 4718596

commit v3 on v2

--- a/solution.py
+++ b/solution.py
@@ -46,10 +46,26 @@
     return high, low, back, np.stack(turn).astype(np.float32), inner
 
 
-def order(step, n_seq):
-    if n_seq % 8:
-        return step
-    return lax.rem(lax.rem(step, 8) * 3, 8) * (n_seq // 8) + step // 8
+def visit(n_seq, place, bit, act):
+    places = n_seq // 2
+    planes = 8 if places % 8 == 0 else 1
+    inner = places // planes
+
+    def group(step, skip):
+        for plane in range(planes):
+            there = place + step + (plane * 3 % planes) * inner
+            there = jnp.where(there >= places, there - places, there)
+            if plane or not skip:
+                act(there, bit)
+            act(there, 1 - bit)
+
+    group(0, True)
+
+    def body(step, carry):
+        group(step, False)
+        return carry
+
+    lax.fori_loop(1, inner, body, 0)
 
 
 def kernel(
@@ -59,13 +75,14 @@
     cot_hbm,
     h_hbm,
     limit_ref,
+    gain_ref,
     high_ref,
     low_ref,
     back_ref,
     turn_ref,
     inner_ref,
     s_final,
-    c_final,
+    z_final,
     z_in,
     gate_in,
     cot_in,
@@ -77,7 +94,8 @@
     s_out,
     c_out,
     s_turned,
-    c_turned,
+    z_turned,
+    g_keep,
     zbuf,
     hbuf,
     m_high,
@@ -108,9 +126,6 @@
     place = seq // 2
     chip = place * 2 + user
 
-    def at_chip(target, which):
-        return {"seq": (target // 2) * 2 + which, "user": lax.rem(target, 2)}
-
     def remote(src, dst, which, device):
         return pltpu.make_async_remote_copy(
             src_ref=src,
@@ -121,35 +136,17 @@
             device_id_type=pl.DeviceIdType.MESH,
         )
 
-    def scatter(which, src, dst):
-        def put(target):
-            remote(src.at[target], dst.at[seq], which, at_chip(target, user)).start()
-
+    def await_all(ref, sem):
+        pltpu.make_async_copy(ref, ref, sem).wait()
+
+    def await_sent(which, some):
         @pl.when(core == user)
         def _():
-            pltpu.make_async_copy(src.at[chip], dst.at[seq], recv_sems.at[which]).start()
+            await_all(some(n_seq - 1), send_sems.at[which])
 
         @pl.when(core != user)
         def _():
-            put(chip)
-
-        def body(step, carry):
-            put(lax.rem(chip + order(step, n_seq), n_seq))
-            return carry
-
-        lax.fori_loop(1, n_seq, body, 0)
-
-    def await_all(ref, sem):
-        pltpu.make_async_copy(ref, ref, sem).wait()
-
-    def await_sent(which, src):
-        @pl.when(core == user)
-        def _():
-            await_all(src.at[pl.ds(0, n_seq - 1)], send_sems.at[which])
-
-        @pl.when(core != user)
-        def _():
-            await_all(src, send_sems.at[which])
+            await_all(some(n_seq), send_sems.at[which])
 
     inputs = [
         pltpu.make_async_copy(z_hbm.at[0], z_in, input_sems.at[0]),
@@ -167,70 +164,124 @@
     for load in inputs + loads:
         load.start()
 
+    barrier = pltpu.get_barrier_semaphore()
+
+    def greet(there, bit):
+        pl.semaphore_signal(
+            barrier,
+            inc=1,
+            device_id={"seq": 2 * there + bit, "user": core},
+            device_id_type=pl.DeviceIdType.MESH,
+        )
+
+    @pl.when(core != user)
+    def _():
+        greet(place, core)
+
+    visit(n_seq, place, core, greet)
+
     channels = PER * n_seq
-    width = min(LANES, channels)
-    columns = channels // width
-
-    def pack(dst):
-        def body(part, carry):
-            tile = stage[pl.ds(pl.multiple_of(part * 16 * SUB * PER * 2, 8), 16 * SUB * PER * 2), :]
-            dst[pl.ds(part * 16, 16)] = tile.reshape(16, PER, 2 * SUB, LANES).astype(jnp.bfloat16)
-            return carry
-
-        lax.fori_loop(0, n_seq // 16, body, 0)
-
     for load in inputs[:3]:
         load.wait()
 
-    def turn_zg(part, carry):
-        at = pl.ds(pl.multiple_of(part * LANES, LANES), LANES)
-        times = seq * (SUB * LANES) + part * LANES
-        times = times + lax.broadcasted_iota(jnp.int32, (LANES, channels), 0)
-        alive = times < limit_ref[0]
-        z = jnp.where(alive, z_in[at, :].astype(jnp.float32), 0.0)
-        g = cot_in[at, :].astype(jnp.float32) * gate_in[at, :].astype(jnp.float32)
-        g = jnp.where(alive, g, 0.0)
-        for column in range(columns):
-            cut = slice(column * width, (column + 1) * width)
-            first = column * width * 2 * SUB + part
-            stage[pl.ds(first, width, stride=2 * SUB), :] = z[:, cut].T
-            stage[pl.ds(first + SUB, width, stride=2 * SUB), :] = g[:, cut].T
-        return carry
-
-    lax.fori_loop(0, SUB, turn_zg, 0)
-    pack(zg_ref)
-    scatter(0, zg_ref, zbuf.at[user])
+    def pack(column, dst):
+        size = n_seq * 2 * SUB // 4
+
+        def body(part, carry):
+            first = pl.multiple_of(column * n_seq * 2 * SUB + part * size, 8)
+            tile = stage[pl.ds(first, size), :].reshape(n_seq // 4, 2 * SUB, LANES)
+            dst[pl.ds(part * (n_seq // 4), n_seq // 4)] = tile.astype(jnp.bfloat16)
+            return carry
+
+        lax.fori_loop(0, 4, body, 0)
+
+    def scatter(which, src, dst):
+        def put(there, bit):
+            to = {"seq": 2 * there + user, "user": bit}
+            remote(src(2 * there + bit), dst, which, to).start()
+
+        @pl.when(core == user)
+        def _():
+            pltpu.make_async_copy(src(chip), dst, recv_sems.at[which]).start()
+
+        @pl.when(core != user)
+        def _():
+            put(place, user)
+
+        visit(n_seq, place, user, put)
+
+    def scatter_zg(which, columns):
+        scatter(which, lambda target: zg_ref.at[columns, target], zbuf.at[user, columns, seq])
+
+    first, others = pl.ds(0, 1), pl.ds(1, PER - 1)
+    for column in range(PER):
+        cut = slice(column * n_seq, (column + 1) * n_seq)
+
+        def turn_zg(part, carry, column=column, cut=cut):
+            at = pl.ds(pl.multiple_of(part * LANES, LANES), LANES)
+            times = seq * (SUB * LANES) + part * LANES
+            times = times + lax.broadcasted_iota(jnp.int32, (LANES, n_seq), 0)
+            alive = times < limit_ref[0]
+            z = jnp.where(alive, z_in[at, cut].astype(jnp.float32), 0.0)
+            g = cot_in[at, cut].astype(jnp.float32) * gate_in[at, cut].astype(jnp.float32)
+            g = jnp.where(alive, g, 0.0)
+            g_keep[at, cut] = g.astype(jnp.bfloat16)
+            top = column * n_seq * 2 * SUB + part
+            stage[pl.ds(top, n_seq, stride=2 * SUB), :] = z.T
+            stage[pl.ds(top + SUB, n_seq, stride=2 * SUB), :] = g.T
+            return carry
+
+        lax.fori_loop(0, SUB, turn_zg, 0)
+        pack(column, zg_ref.at[column])
+        if column == 0:
+
+            @pl.when(core == user)
+            def _():
+                pl.semaphore_wait(barrier, n_seq - 1)
+
+            @pl.when(core != user)
+            def _():
+                pl.semaphore_wait(barrier, n_seq)
+
+            scatter_zg(0, first)
+    scatter_zg(1, others)
 
     inputs[3].wait()
-    for kind in range(2):
-        for column in range(columns):
-            cut = slice(column * width, (column + 1) * width)
-            wide[column, :, :width] = h_in[kind, :, cut].astype(jnp.float32)
-
-        def turn_h(low_bits, carry, kind=kind):
-            for column in range(columns):
-                tile = wide[column, pl.ds(low_bits, LANES, stride=SUB), :]
-                first = column * width * 2 * SUB + kind * SUB + low_bits
-                stage[pl.ds(first, width, stride=2 * SUB), :] = tile.T[:width]
+    for column in range(PER):
+        cut = slice(column * n_seq, (column + 1) * n_seq)
+        for kind in range(2):
+            wide[kind, :, :n_seq] = h_in[kind, :, cut].astype(jnp.float32)
+
+        def turn_h(low_bits, carry, column=column):
+            for kind in range(2):
+                tile = wide[kind, pl.ds(low_bits, LANES, stride=SUB), :]
+                first = column * n_seq * 2 * SUB + kind * SUB + low_bits
+                stage[pl.ds(first, n_seq, stride=2 * SUB), :] = tile.T[:n_seq]
             return carry
 
         lax.fori_loop(0, SUB, turn_h, 0)
-    pack(h_ref)
-    scatter(1, h_ref, hbuf)
+        pack(column, h_ref.at[:, column])
+    scatter(3, lambda target: h_ref.at[target], hbuf.at[seq])
 
     for load in loads:
         load.wait()
 
     mate = {"seq": seq + 1 - 2 * core, "user": user}
-    await_all(zbuf.at[core], recv_sems.at[0])
-    swap = remote(zbuf.at[core], zbuf.at[core], 2, mate)
-    swap.start()
-    swap.wait()
 
     def forward(channel, carry):
+        for which, columns in ((0, first), (1, others)):
+
+            @pl.when(channel == which)
+            def _(which=which, columns=columns):
+                arrived = zbuf.at[core, columns]
+                await_all(arrived, recv_sems.at[which])
+                swap = remote(arrived, arrived, 4 + which, mate)
+                swap.start()
+                swap.wait()
+
         def fill(part, inner_carry):
             for who in range(2):
-                tile = zbuf[who, pl.ds(part * groups, groups), channel]
+                tile = zbuf[who, channel, pl.ds(part * groups, groups)]
                 tile = tile.astype(jnp.float32)
                 at = pl.ds(pl.multiple_of(part * block, block), block)
                 for kind in range(2):
@@ -287,24 +338,20 @@
 
     slot = core * n_seq + chip
 
-    def put_s(step):
-        target = lax.rem(chip + order(step // 2, n_seq), n_seq)
-        which = lax.rem(step, 2)
-        owner = (target // 2) * 2 + which
-        there = lax.rem(target, 2)
-        src = s_send.at[there * n_seq + owner]
-        remote(src, s_out.at[slot], 3, {"seq": owner, "user": there}).start()
-
-    pltpu.make_async_copy(s_send.at[user * n_seq + seq], s_out.at[slot], recv_sems.at[3]).start()
-    put_s(1 - core)
-
-    def body_s(step, carry):
-        put_s(step)
-        return carry
-
-    lax.fori_loop(2, 2 * n_seq, body_s, 0)
-
-    await_all(hbuf, recv_sems.at[1])
+    def put_s(there, bit, other):
+        owner = 2 * there + other
+        src = s_send.at[bit * n_seq + owner]
+        remote(src, s_out.at[slot], 7, {"seq": owner, "user": bit}).start()
+
+    def put_both(there, bit):
+        put_s(there, bit, 0)
+        put_s(there, bit, 1)
+
+    pltpu.make_async_copy(s_send.at[user * n_seq + seq], s_out.at[slot], recv_sems.at[7]).start()
+    put_s(place, user, 1 - core)
+    visit(n_seq, place, user, put_both)
+
+    await_all(hbuf, recv_sems.at[3])
 
     def inverse(channel, carry):
         dot = functools.partial(jnp.dot, preferred_element_type=jnp.float32)
@@ -351,7 +398,7 @@
 
     lax.fori_loop(0, PER, inverse, 0)
 
-    swap_back = remote(c_part.at[1 - core], c_other, 4, mate)
+    swap_back = remote(c_part.at[1 - core], c_other, 8, mate)
     swap_back.start()
     swap_back.wait()
 
@@ -362,92 +409,99 @@
 
     lax.fori_loop(0, blocks, join, 0)
 
-    def put_c(target):
-        remote(c_send.at[target], c_out.at[chip], 5, {"seq": target, "user": core}).start()
+    def put_c(there, bit):
+        target = 2 * there + bit
+        remote(c_send.at[target], c_out.at[chip], 9, {"seq": target, "user": core}).start()
 
     @pl.when(core == user)
     def _():
-        pltpu.make_async_copy(c_send.at[seq], c_out.at[chip], recv_sems.at[5]).start()
+        pltpu.make_async_copy(c_send.at[seq], c_out.at[chip], recv_sems.at[9]).start()
 
     @pl.when(core != user)
     def _():
-        put_c(seq)
-
-    def body_c(step, carry):
-        put_c(lax.rem(seq + order(step, n_seq), n_seq))
-        return carry
-
-    lax.fori_loop(1, n_seq, body_c, 0)
-
-    def unpack(src):
+        put_c(place, core)
+
+    visit(n_seq, place, core, put_c)
+
+    def unpack(column, src):
+        size = n_seq * SUB // 4
+
         def body(part, carry):
-            tile = src[pl.ds(part * 16, 16)].astype(jnp.float32)
-            size = 16 * PER * SUB
-            stage[pl.ds(pl.multiple_of(part * size, 8), size), :] = tile.reshape(size, LANES)
+            tile = src[pl.ds(part * (n_seq // 4), n_seq // 4)].astype(jnp.float32)
+            first = pl.multiple_of(column * n_seq * SUB + part * size, 8)
+            stage[pl.ds(first, size), :] = tile.reshape(size, LANES)
             return carry
 
-        lax.fori_loop(0, n_seq // 16, body, 0)
+        lax.fori_loop(0, 4, body, 0)
 
     half = LANES // 2
-    await_all(s_out, recv_sems.at[3])
+    await_all(s_out, recv_sems.at[7])
     for parity in range(2):
-        unpack(s_out.at[pl.ds(parity * n_seq, n_seq)])
-
-        def turn_s(low_bits, carry):
-            for column in range(columns):
-                first = column * width * SUB + low_bits
-                tile = stage[pl.ds(first, width, stride=SUB), :].T
+        for column in range(PER):
+            cut = slice(column * n_seq, (column + 1) * n_seq)
+            unpack(column, s_out.at[pl.ds(parity * n_seq, n_seq), column])
+
+            def turn_s(low_bits, carry, column=column):
+                first = column * n_seq * SUB + low_bits
+                tile = stage[pl.ds(first, n_seq, stride=SUB), :].T
                 for kind in range(2):
+                    piece = tile[kind * half : (kind + 1) * half]
                     first = kind * half * SUB + low_bits
-                    piece = tile[kind * half : (kind + 1) * half]
-                    wide[column, pl.ds(first, half, stride=SUB), :width] = piece
-            return carry
-
-        lax.fori_loop(0, SUB, turn_s, 0)
-        for column in range(columns):
-            cut = slice(column * width, (column + 1) * width)
+                    wide[column, pl.ds(first, half, stride=SUB), :n_seq] = piece
+                return carry
+
+            lax.fori_loop(0, SUB, turn_s, 0)
             for kind in range(2):
                 at = pl.ds(kind * half * SUB, half * SUB)
-                s_turned[parity, kind, :, cut] = wide[column, at, :width].astype(jnp.bfloat16)
+                s_turned[parity, kind, :, cut] = wide[column, at, :n_seq].astype(jnp.bfloat16)
     s_store = pltpu.make_async_copy(s_turned, s_final, input_sems.at[0])
     s_store.start()
 
-    await_all(c_out, recv_sems.at[5])
-    unpack(c_out)
-
-    def turn_c(part, carry):
+    await_all(c_out, recv_sems.at[9])
+    for column in range(PER):
+        unpack(column, c_out.at[:, column])
+
+    def finish(part, carry):
         at = pl.ds(pl.multiple_of(part * LANES, LANES), LANES)
-        for column in range(columns):
-            first = column * width * SUB + part
-            tile = stage[pl.ds(first, width, stride=SUB), :].T
-            c_turned[at, column * width : (column + 1) * width] = tile.astype(jnp.bfloat16)
+        times = seq * (SUB * LANES) + part * LANES
+        times = times + lax.broadcasted_iota(jnp.int32, (LANES, n_seq), 0)
+        alive = times < limit_ref[0]
+        for column in range(PER):
+            cut = slice(column * n_seq, (column + 1) * n_seq)
+            conv = stage[pl.ds(column * n_seq * SUB + part, n_seq, stride=SUB), :].T
+            total = gain_ref[:, cut] * g_keep[at, cut].astype(jnp.float32) + conv
+            z_turned[at, cut] = jnp.where(alive, total, 0.0).astype(jnp.bfloat16)
         return carry
 
-    lax.fori_loop(0, SUB, turn_c, 0)
-    c_store = pltpu.make_async_copy(c_turned, c_final, input_sems.at[1])
-    c_store.start()
-
-    await_sent(0, zg_ref)
-    await_sent(1, h_ref)
-    await_all(s_send.at[pl.ds(0, 2 * n_seq - 1)], send_sems.at[3])
-    await_sent(5, c_send)
+    lax.fori_loop(0, SUB, finish, 0)
+    z_store = pltpu.make_async_copy(z_turned, z_final.at[0], input_sems.at[1])
+    z_store.start()
+
+    await_sent(0, lambda count: zg_ref.at[first, pl.ds(0, count)])
+    await_sent(1, lambda count: zg_ref.at[others, pl.ds(0, count)])
+    await_sent(3, lambda count: h_ref.at[pl.ds(0, count)])
+    await_all(s_send.at[pl.ds(0, 2 * n_seq - 1)], send_sems.at[7])
+    await_sent(9, lambda count: c_send.at[pl.ds(0, count)])
     s_store.wait()
-    c_store.wait()
-
-
-def mixer(n_seq, z_input, gate_input, cotangent, spectrum, lengths):
+    z_store.wait()
+
+
+def mixer(n_seq, z_input, gate_input, cotangent, spectrum, skip_gain, lengths):
     rows = SUB * n_seq
     span, channels = z_input.shape[1:]
     bf16, f32 = jnp.bfloat16, jnp.float32
     high, low, back, turn, inner = (jnp.asarray(t) for t in tables(n_seq))
+    gain = skip_gain.reshape(1, channels)
     anywhere = pl.BlockSpec(memory_space=pl.ANY)
     return pl.pallas_call(
         functools.partial(kernel, n_seq),
         out_shape=(
             jax.ShapeDtypeStruct((2, 2, span // 2, channels), bf16),
-            jax.ShapeDtypeStruct((span, channels), bf16),
+            jax.ShapeDtypeStruct((1, span, channels), bf16),
         ),
-        in_specs=[anywhere] * 4 + [pl.BlockSpec(memory_space=pltpu.SMEM)] + [anywhere] * 5,
+        in_specs=[anywhere] * 4
+        + [pl.BlockSpec(memory_space=pltpu.SMEM), pl.BlockSpec(memory_space=pltpu.VMEM)]
+        + [anywhere] * 5,
         out_specs=(anywhere, anywhere),
         scratch_shapes=[
             pltpu.VMEM((span, channels), bf16),
@@ -455,14 +509,15 @@
             pltpu.VMEM((span, channels), bf16),
             pltpu.VMEM((2, span, channels), bf16),
             pltpu.VMEM((channels * 2 * SUB, LANES), f32),
-            pltpu.VMEM((max(1, channels // LANES), span, LANES), f32),
-            pltpu.VMEM((n_seq, PER, 2 * SUB, LANES), bf16),
+            pltpu.VMEM((PER, span, LANES), f32),
+            pltpu.VMEM((PER, n_seq, 2 * SUB, LANES), bf16),
             pltpu.VMEM((n_seq, PER, 2 * SUB, LANES), bf16),
             pltpu.VMEM((2 * n_seq, PER, SUB, LANES), bf16),
             pltpu.VMEM((n_seq, PER, SUB, LANES), bf16),
             pltpu.VMEM((2, 2, span // 2, channels), bf16),
             pltpu.VMEM((span, channels), bf16),
-            pltpu.VMEM((2, n_seq, PER, 2 * SUB, LANES), bf16),
+            pltpu.VMEM((span, channels), bf16),
+            pltpu.VMEM((2, PER, n_seq, 2 * SUB, LANES), bf16),
             pltpu.VMEM((n_seq, PER, 2 * SUB, LANES), bf16),
             pltpu.VMEM((2 * rows, rows), bf16),
             pltpu.VMEM((2 * rows, rows), bf16),
@@ -478,25 +533,21 @@
             pltpu.VMEM((n_seq, PER, SUB, LANES), bf16),
             pltpu.SemaphoreType.DMA((4,)),
             pltpu.SemaphoreType.DMA((5,)),
-            pltpu.SemaphoreType.DMA((6,)),
-            pltpu.SemaphoreType.DMA((6,)),
+            pltpu.SemaphoreType.DMA((10,)),
+            pltpu.SemaphoreType.DMA((10,)),
         ],
         compiler_params=pltpu.CompilerParams(
-            has_side_effects=True, vmem_limit_bytes=60 * 1024 * 1024
+            collective_id=0, has_side_effects=True, vmem_limit_bytes=60 * 1024 * 1024
         ),
-    )(z_input, gate_input, cotangent, spectrum, lengths, high, low, back, turn, inner)
+    )(z_input, gate_input, cotangent, spectrum, lengths, gain, high, low, back, turn, inner)
 
 
 def on_device(z_input, gate_input, cotangent, spectrum, skip_gain, lengths):
     n_seq = lax.axis_size("seq")
-    span = z_input.shape[1]
-    times = lax.axis_index("seq") * span + jnp.arange(span, dtype=jnp.int32)
-    alive = (times < lengths[0])[:, None]
-    s_rows, conv = mixer(n_seq, z_input, gate_input, cotangent, spectrum, lengths)
-    product = cotangent[0].astype(jnp.float32) * gate_input[0].astype(jnp.float32)
-    grad = product.astype(jnp.bfloat16).astype(jnp.float32)
-    z_grad = jnp.where(alive, skip_gain * grad + conv.astype(jnp.float32), 0.0)
-    return (z_grad.astype(jnp.bfloat16)[None], s_rows.astype(jnp.float32)[:, :, None])
+    s_rows, z_grad = mixer(
+        n_seq, z_input, gate_input, cotangent, spectrum, skip_gain, lengths
+    )
+    return (z_grad, s_rows.astype(jnp.float32)[:, :, None])
 
 
 def solution(mesh):

time: 152 us -> 144 us (0.947)
  Pallas kernels: 146 us -> 137 us
  local copies, waits for them, and re-layouts: 0.02 us -> 2.13 us
    pallas_call x1, Pallas kernels: 146 us -> 137 us  [mixer(): pl.pallas_call(functools.partial(kernel, n_seq), out_shape=(jax.ShapeDtyp...]
    broadcast_in_dim x1 -> x0, other arithmetic: 2.55 us -> none  [on_device(): z_grad.astype(jnp.bfloat16)[None]]
where the time goes in v3:
time: 144 us
  Pallas kernels  137 us (95%)
  other arithmetic  3.35 us (2%)
  local copies, waits for them, and re-layouts  2.13 us (1%)
    pallas_call x1, Pallas kernels, mixer(): pl.pallas_call(functools.partial(kernel, n_seq), out_shape=(jax.ShapeDtyp...  137 us
    unnamed x1, other arithmetic  3.35 us

profile of v3, /device:TPU:7, one launch (start us, length us, event | category | flops | bytes accessed | tf_op | source)
XLA Modules:
  0.0 144.1 jit_solution(14963120717890984954)
XLA Ops:
  1.3 1.2 reshape.7.gain_ref
  2.5 137.4 %shard_map.122 = (bf16[2,2,512,384]{3,2,1,0:T(8,128)(2,1)}, bf16[1,1024,384]{2,1,0:T(8,128)(2,1)}) custom-call(bf16[1,1024,384]{2,1,0:T(8,128)(2,1)} %z_hbm.1, bf16[1,1024,384]{2,1,0:T(8,128)(2,1)} %gate_hbm.1, bf16[1,1024,384]{2,1,0:T(8,128)(2,1)} %cot_hbm.1, bf16[2,2,1,1024,384]{4,3,2,1,0:T(8,128)(2,1)} %h_hbm.1, s32[1]{0:T(128)S(6)} %copy.15.limit_ref, ...), custom_call_target="tpu_custom_call" | custom-call | tf_op jit(solution)/shard_map/pallas_call | solution.py:496
  139.9 0.0 copy-start
  139.9 3.3 %bitcast_convert_fusion = f32[2,2,1,512,384]{4,3,2,1,0:T(8,128)} fusion(bf16[2,2,512,384]{3,2,1,0:T(8,128)(2,1)} %get-tuple-element.5), kind=kLoop, calls=%fused_computation | loop fusion | flops 786432 | bytes 4718592
  143.2 0.0 copy-done
  143.3 0.9 copy.16
Async XLA Ops:
  139.9 3.4 %copy-start = (bf16[1,1024,384]{2,1,0:T(8,128)(2,1)S(1)}, bf16[1,1024,384]{2,1,0:T(8,128)(2,1)}, u32[]{:S(2)}) copy-start(bf16[1,1024,384]{2,1,0:T(8,128)(2,1)} %get-tuple-element.10) | copy-start | bytes 2359300

commit v4 on v3

--- a/solution.py
+++ b/solution.py
@@ -93,8 +93,6 @@
     h_ref,
     s_out,
     c_out,
-    s_turned,
-    z_turned,
     g_keep,
     zbuf,
     hbuf,
@@ -107,6 +105,7 @@
     g_buf,
     b_buf,
     s_send,
+    s_cross,
     c_part,
     c_other,
     c_send,
@@ -210,10 +209,6 @@
 
         visit(n_seq, place, user, put)
 
-    def scatter_zg(which, columns):
-        scatter(which, lambda target: zg_ref.at[columns, target], zbuf.at[user, columns, seq])
-
-    first, others = pl.ds(0, 1), pl.ds(1, PER - 1)
     for column in range(PER):
         cut = slice(column * n_seq, (column + 1) * n_seq)
 
@@ -232,19 +227,17 @@
             return carry
 
         lax.fori_loop(0, SUB, turn_zg, 0)
-        pack(column, zg_ref.at[column])
-        if column == 0:
-
-            @pl.when(core == user)
-            def _():
-                pl.semaphore_wait(barrier, n_seq - 1)
-
-            @pl.when(core != user)
-            def _():
-                pl.semaphore_wait(barrier, n_seq)
-
-            scatter_zg(0, first)
-    scatter_zg(1, others)
+        pack(column, zg_ref.at[:, column])
+
+    @pl.when(core == user)
+    def _():
+        pl.semaphore_wait(barrier, n_seq - 1)
+
+    @pl.when(core != user)
+    def _():
+        pl.semaphore_wait(barrier, n_seq)
+
+    scatter(0, lambda target: zg_ref.at[target], zbuf.at[user, seq])
 
     inputs[3].wait()
     for column in range(PER):
@@ -268,20 +261,19 @@
 
     mate = {"seq": seq + 1 - 2 * core, "user": user}
 
+    arrived = zbuf.at[core]
+    await_all(arrived, recv_sems.at[0])
+    swap = remote(arrived, arrived, 1, mate)
+    swap.start()
+    swap.wait()
+
+    def cross(channel):
+        return remote(s_cross.at[channel], s_send.at[:, core, channel], 4 + channel, mate)
+
     def forward(channel, carry):
-        for which, columns in ((0, first), (1, others)):
-
-            @pl.when(channel == which)
-            def _(which=which, columns=columns):
-                arrived = zbuf.at[core, columns]
-                await_all(arrived, recv_sems.at[which])
-                swap = remote(arrived, arrived, 4 + which, mate)
-                swap.start()
-                swap.wait()
-
         def fill(part, inner_carry):
             for who in range(2):
-                tile = zbuf[who, channel, pl.ds(part * groups, groups)]
+                tile = zbuf[who, pl.ds(part * groups, groups), channel]
                 tile = tile.astype(jnp.float32)
                 at = pl.ds(pl.multiple_of(part * block, block), block)
                 for kind in range(2):
@@ -324,32 +316,41 @@
                 s_imag = c_imag if who == 0 else s_imag + c_imag
             s_real, s_imag = s_real * scale, s_imag * scale
             half = LANES // 2
+            outs = []
             for who in range(2):
                 cut = slice(who * half, (who + 1) * half)
                 out = jnp.concatenate([s_real[:, cut], s_imag[:, cut]], axis=1)
-                out = out.reshape(groups, SUB, LANES).astype(jnp.bfloat16)
-                s_send[pl.ds(who * n_seq + part * groups, groups), channel] = out
+                outs.append(out.reshape(groups, SUB, LANES))
+            here = pl.ds(part * groups, groups)
+            s_send[here, core, channel] = jnp.where(core == 0, outs[0], outs[1]).astype(jnp.bfloat16)
+            s_cross[channel, here] = jnp.where(core == 0, outs[1], outs[0]).astype(jnp.bfloat16)
             return inner_carry
 
         lax.fori_loop(0, blocks, spectrum, 0)
+        cross(channel).start()
         return carry
 
     lax.fori_loop(0, PER, forward, 0)
 
-    slot = core * n_seq + chip
-
-    def put_s(there, bit, other):
-        owner = 2 * there + other
-        src = s_send.at[bit * n_seq + owner]
-        remote(src, s_out.at[slot], 7, {"seq": owner, "user": bit}).start()
-
-    def put_both(there, bit):
-        put_s(there, bit, 0)
-        put_s(there, bit, 1)
-
-    pltpu.make_async_copy(s_send.at[user * n_seq + seq], s_out.at[slot], recv_sems.at[7]).start()
-    put_s(place, user, 1 - core)
-    visit(n_seq, place, user, put_both)
+    for channel in range(PER):
+        cross(channel).wait()
+
+    def gather(which, src, dst):
+        def put(there, bit):
+            to = {"seq": 2 * there + bit, "user": core}
+            remote(src.at[2 * there + bit], dst.at[chip], which, to).start()
+
+        @pl.when(core == user)
+        def _():
+            pltpu.make_async_copy(src.at[seq], dst.at[chip], recv_sems.at[which]).start()
+
+        @pl.when(core != user)
+        def _():
+            put(place, core)
+
+        visit(n_seq, place, core, put)
+
+    gather(7, s_send, s_out)
 
     await_all(hbuf, recv_sems.at[3])
 
@@ -409,19 +410,7 @@
 
     lax.fori_loop(0, blocks, join, 0)
 
-    def put_c(there, bit):
-        target = 2 * there + bit
-        remote(c_send.at[target], c_out.at[chip], 9, {"seq": target, "user": core}).start()
-
-    @pl.when(core == user)
-    def _():
-        pltpu.make_async_copy(c_send.at[seq], c_out.at[chip], recv_sems.at[9]).start()
-
-    @pl.when(core != user)
-    def _():
-        put_c(place, core)
-
-    visit(n_seq, place, core, put_c)
+    gather(9, c_send, c_out)
 
     def unpack(column, src):
         size = n_seq * SUB // 4
@@ -439,7 +428,7 @@
     for parity in range(2):
         for column in range(PER):
             cut = slice(column * n_seq, (column + 1) * n_seq)
-            unpack(column, s_out.at[pl.ds(parity * n_seq, n_seq), column])
+            unpack(column, s_out.at[:, parity, column])
 
             def turn_s(low_bits, carry, column=column):
                 first = column * n_seq * SUB + low_bits
@@ -453,9 +442,7 @@
             lax.fori_loop(0, SUB, turn_s, 0)
             for kind in range(2):
                 at = pl.ds(kind * half * SUB, half * SUB)
-                s_turned[parity, kind, :, cut] = wide[column, at, :n_seq].astype(jnp.bfloat16)
-    s_store = pltpu.make_async_copy(s_turned, s_final, input_sems.at[0])
-    s_store.start()
+                s_final[parity, kind, :, cut] = wide[column, at, :n_seq].astype(jnp.bfloat16)
 
     await_all(c_out, recv_sems.at[9])
     for column in range(PER):
@@ -469,21 +456,16 @@
         for column in range(PER):
             cut = slice(column * n_seq, (column + 1) * n_seq)
             conv = stage[pl.ds(column * n_seq * SUB + part, n_seq, stride=SUB), :].T
-            total = gain_ref[:, cut] * g_keep[at, cut].astype(jnp.float32) + conv
-            z_turned[at, cut] = jnp.where(alive, total, 0.0).astype(jnp.bfloat16)
+            total = gain_ref[cut][None, :] * g_keep[at, cut].astype(jnp.float32) + conv
+            z_final[0, at, cut] = jnp.where(alive, total, 0.0).astype(jnp.bfloat16)
         return carry
 
     lax.fori_loop(0, SUB, finish, 0)
-    z_store = pltpu.make_async_copy(z_turned, z_final.at[0], input_sems.at[1])
-    z_store.start()
-
-    await_sent(0, lambda count: zg_ref.at[first, pl.ds(0, count)])
-    await_sent(1, lambda count: zg_ref.at[others, pl.ds(0, count)])
+
+    await_sent(0, lambda count: zg_ref.at[pl.ds(0, count)])
     await_sent(3, lambda count: h_ref.at[pl.ds(0, count)])
-    await_all(s_send.at[pl.ds(0, 2 * n_seq - 1)], send_sems.at[7])
+    await_sent(7, lambda count: s_send.at[pl.ds(0, count)])
     await_sent(9, lambda count: c_send.at[pl.ds(0, count)])
-    s_store.wait()
-    z_store.wait()
 
 
 def mixer(n_seq, z_input, gate_input, cotangent, spectrum, skip_gain, lengths):
@@ -491,18 +473,17 @@
     span, channels = z_input.shape[1:]
     bf16, f32 = jnp.bfloat16, jnp.float32
     high, low, back, turn, inner = (jnp.asarray(t) for t in tables(n_seq))
-    gain = skip_gain.reshape(1, channels)
     anywhere = pl.BlockSpec(memory_space=pl.ANY)
     return pl.pallas_call(
         functools.partial(kernel, n_seq),
         out_shape=(
-            jax.ShapeDtypeStruct((2, 2, span // 2, channels), bf16),
-            jax.ShapeDtypeStruct((1, span, channels), bf16),
+            pltpu.VMEM((2, 2, span // 2, channels), bf16),
+            pltpu.VMEM((1, span, channels), bf16),
         ),
         in_specs=[anywhere] * 4
         + [pl.BlockSpec(memory_space=pltpu.SMEM), pl.BlockSpec(memory_space=pltpu.VMEM)]
         + [anywhere] * 5,
-        out_specs=(anywhere, anywhere),
+        out_specs=(pl.BlockSpec(memory_space=pltpu.VMEM),) * 2,
         scratch_shapes=[
             pltpu.VMEM((span, channels), bf16),
             pltpu.VMEM((span, channels), bf16),
@@ -510,14 +491,12 @@
             pltpu.VMEM((2, span, channels), bf16),
             pltpu.VMEM((channels * 2 * SUB, LANES), f32),
             pltpu.VMEM((PER, span, LANES), f32),
-            pltpu.VMEM((PER, n_seq, 2 * SUB, LANES), bf16),
             pltpu.VMEM((n_seq, PER, 2 * SUB, LANES), bf16),
-            pltpu.VMEM((2 * n_seq, PER, SUB, LANES), bf16),
+            pltpu.VMEM((n_seq, PER, 2 * SUB, LANES), bf16),
+            pltpu.VMEM((n_seq, 2, PER, SUB, LANES), bf16),
             pltpu.VMEM((n_seq, PER, SUB, LANES), bf16),
-            pltpu.VMEM((2, 2, span // 2, channels), bf16),
             pltpu.VMEM((span, channels), bf16),
-            pltpu.VMEM((span, channels), bf16),
-            pltpu.VMEM((2, PER, n_seq, 2 * SUB, LANES), bf16),
+            pltpu.VMEM((2, n_seq, PER, 2 * SUB, LANES), bf16),
             pltpu.VMEM((n_seq, PER, 2 * SUB, LANES), bf16),
             pltpu.VMEM((2 * rows, rows), bf16),
             pltpu.VMEM((2 * rows, rows), bf16),
@@ -527,7 +506,8 @@
             pltpu.VMEM((rows, 4 * LANES), bf16),
             pltpu.VMEM((PER, 2, rows, 2 * LANES), f32),
             pltpu.VMEM((2 * rows, 2 * LANES), bf16),
-            pltpu.VMEM((2 * n_seq, PER, SUB, LANES), bf16),
+            pltpu.VMEM((n_seq, 2, PER, SUB, LANES), bf16),
+            pltpu.VMEM((PER, n_seq, SUB, LANES), bf16),
             pltpu.VMEM((2, n_seq, PER, SUB, LANES), f32),
             pltpu.VMEM((n_seq, PER, SUB, LANES), f32),
             pltpu.VMEM((n_seq, PER, SUB, LANES), bf16),
@@ -537,9 +517,9 @@
             pltpu.SemaphoreType.DMA((10,)),
         ],
         compiler_params=pltpu.CompilerParams(
-            collective_id=0, has_side_effects=True, vmem_limit_bytes=60 * 1024 * 1024
+            collective_id=0, has_side_effects=True, vmem_limit_bytes=56 * 1024 * 1024
         ),
-    )(z_input, gate_input, cotangent, spectrum, lengths, gain, high, low, back, turn, inner)
+    )(z_input, gate_input, cotangent, spectrum, lengths, skip_gain, high, low, back, turn, inner)
 
 
 def on_device(z_input, gate_input, cotangent, spectrum, skip_gain, lengths):

time: 144 us -> 141 us (0.979)
  other arithmetic: 3.35 us -> 1.87 us
    unnamed x1, other arithmetic: 3.35 us -> 1.87 us
where the time goes in v4:
time: 141 us
  Pallas kernels  137 us (97%)
  other arithmetic  1.87 us (1%)
    pallas_call x1, Pallas kernels, mixer(): pl.pallas_call(functools.partial(kernel, n_seq), out_shape=(pltpu.VMEM((2...  137 us

profile of v4, /device:TPU:7, one launch (start us, length us, event | category | flops | bytes accessed | tf_op | source)
XLA Modules:
  0.0 140.6 jit_solution(18394244288060447486)
XLA Ops:
  1.3 136.6 %shard_map.122 = (bf16[2,2,512,384]{3,2,1,0:T(8,128)(2,1)S(1)}, bf16[1,1024,384]{2,1,0:T(8,128)(2,1)S(1)}) custom-call(bf16[1,1024,384]{2,1,0:T(8,128)(2,1)} %z_hbm.1, bf16[1,1024,384]{2,1,0:T(8,128)(2,1)} %gate_hbm.1, bf16[1,1024,384]{2,1,0:T(8,128)(2,1)} %cot_hbm.1, bf16[2,2,1,1024,384]{4,3,2,1,0:T(8,128)(2,1)} %h_hbm.1, s32[1]{0:T(128)S(6)} %copy.16.limit_ref, ...), custom_call_target="tpu_custom_call" | custom-call | tf_op jit(solution)/shard_map/pallas_call | solution.py:477
  137.9 0.9 copy.15
  138.8 1.9 %bitcast_convert_fusion = f32[2,2,1,512,384]{4,3,2,1,0:T(8,128)} fusion(bf16[2,2,512,384]{3,2,1,0:T(8,128)(2,1)S(1)} %get-tuple-element.5), kind=kLoop, calls=%fused_computation | loop fusion | flops 786432 | bytes 4718592

commit v5 on v4

--- a/solution.py
+++ b/solution.py
@@ -160,7 +160,7 @@
         pltpu.make_async_copy(turn_ref.at[core], m_turn, table_sems.at[3]),
         pltpu.make_async_copy(inner_ref, m_inner, table_sems.at[4]),
     ]
-    for load in inputs + loads:
+    for load in inputs[:3]:
         load.start()
 
     barrier = pltpu.get_barrier_semaphore()
@@ -178,6 +178,8 @@
         greet(place, core)
 
     visit(n_seq, place, core, greet)
+    for load in inputs[3:] + loads:
+        load.start()
 
     channels = PER * n_seq
     for load in inputs[:3]:
@@ -442,7 +444,7 @@
             lax.fori_loop(0, SUB, turn_s, 0)
             for kind in range(2):
                 at = pl.ds(kind * half * SUB, half * SUB)
-                s_final[parity, kind, :, cut] = wide[column, at, :n_seq].astype(jnp.bfloat16)
+                s_final[parity, kind, 0, :, cut] = wide[column, at, :n_seq]
 
     await_all(c_out, recv_sems.at[9])
     for column in range(PER):
@@ -477,7 +479,7 @@
     return pl.pallas_call(
         functools.partial(kernel, n_seq),
         out_shape=(
-            pltpu.VMEM((2, 2, span // 2, channels), bf16),
+            pltpu.VMEM((2, 2, 1, span // 2, channels), f32),
             pltpu.VMEM((1, span, channels), bf16),
         ),
         in_specs=[anywhere] * 4
@@ -517,9 +519,33 @@
             pltpu.SemaphoreType.DMA((10,)),
         ],
         compiler_params=pltpu.CompilerParams(
-            collective_id=0, has_side_effects=True, vmem_limit_bytes=56 * 1024 * 1024
+            collective_id=0, has_side_effects=True, vmem_limit_bytes=52 * 1024 * 1024
         ),
     )(z_input, gate_input, cotangent, spectrum, lengths, skip_gain, high, low, back, turn, inner)
+
+
+def store(s_ref, z_ref, s_out, z_out, sems):
+    copies = [pltpu.make_async_copy(z_ref, z_out, sems.at[4])]
+    for parity in range(2):
+        for kind in range(2):
+            src, dst = s_ref.at[parity, kind], s_out.at[parity, kind]
+            copies.append(pltpu.make_async_copy(src, dst, sems.at[2 * parity + kind]))
+    for copy in copies:
+        copy.start()
+    for copy in copies:
+        copy.wait()
+
+
+def settle(s_rows, z_grad):
+    held = [pltpu.with_memory_space_constraint(a, pltpu.VMEM) for a in (s_rows, z_grad)]
+    return pl.pallas_call(
+        store,
+        out_shape=tuple(jax.ShapeDtypeStruct(a.shape, a.dtype) for a in (s_rows, z_grad)),
+        in_specs=[pl.BlockSpec(memory_space=pl.ANY)] * 2,
+        out_specs=(pl.BlockSpec(memory_space=pltpu.HBM),) * 2,
+        scratch_shapes=[pltpu.SemaphoreType.DMA((5,))],
+        compiler_params=pltpu.CompilerParams(vmem_limit_bytes=4 * 1024 * 1024),
+    )(*held)
 
 
 def on_device(z_input, gate_input, cotangent, spectrum, skip_gain, lengths):
@@ -527,7 +553,8 @@
     s_rows, z_grad = mixer(
         n_seq, z_input, gate_input, cotangent, spectrum, skip_gain, lengths
     )
-    return (z_grad, s_rows.astype(jnp.float32)[:, :, None])
+    spectrum_grad, z_grad = settle(s_rows, z_grad)
+    return (z_grad, spectrum_grad)
 
 
 def solution(mesh):

time: 141 us -> 140 us (level)
  Pallas kernels: 137 us -> 139 us
  other arithmetic: 1.87 us -> 0 us
    pallas_call x0 -> x1, Pallas kernels: none -> 1.96 us  [settle(): pl.pallas_call(store, out_shape=tuple((jax.ShapeDtypeStruct(a.shape, a.dt...]
    unnamed x1 -> x0, other arithmetic: 1.87 us -> none
where the time goes in v5:
time: 140 us
  Pallas kernels  139 us (99%)
    pallas_call x1, Pallas kernels, mixer(): pl.pallas_call(functools.partial(kernel, n_seq), out_shape=(pltpu.VMEM((2...  137 us

profile of v5, /device:TPU:7, one launch (start us, length us, event | category | flops | bytes accessed | tf_op | source)
XLA Modules:
  0.0 139.8 jit_solution(12517371162240285521)
XLA Ops:
  1.3 136.6 %shard_map.122 = (f32[2,2,1,512,384]{4,3,2,1,0:T(8,128)S(1)}, bf16[1,1024,384]{2,1,0:T(8,128)(2,1)S(1)}) custom-call(bf16[1,1024,384]{2,1,0:T(8,128)(2,1)} %z_hbm.1, bf16[1,1024,384]{2,1,0:T(8,128)(2,1)} %gate_hbm.1, bf16[1,1024,384]{2,1,0:T(8,128)(2,1)} %cot_hbm.1, bf16[2,2,1,1024,384]{4,3,2,1,0:T(8,128)(2,1)} %h_hbm.1, s32[1]{0:T(128)S(6)} %copy.13.limit_ref, ...), custom_call_target="tpu_custom_call" | custom-call | tf_op jit(solution)/shard_map/pallas_call | solution.py:479
  137.8 2.0 %shard_map.123 = (f32[2,2,1,512,384]{4,3,2,1,0:T(8,128)}, bf16[1,1024,384]{2,1,0:T(8,128)(2,1)}) custom-call(f32[2,2,1,512,384]{4,3,2,1,0:T(8,128)S(1)} %get-tuple-element.6.s_ref, bf16[1,1024,384]{2,1,0:T(8,128)(2,1)S(1)} %get-tuple-element.7.z_ref), custom_call_target="tpu_custom_call" | custom-call | tf_op jit(solution)/shard_map/pallas_call | solution.py:541

commit v6 on v5

--- a/solution.py
+++ b/solution.py
@@ -245,7 +245,7 @@
     for column in range(PER):
         cut = slice(column * n_seq, (column + 1) * n_seq)
         for kind in range(2):
-            wide[kind, :, :n_seq] = h_in[kind, :, cut].astype(jnp.float32)
+            wide[kind, : SUB * LANES, :n_seq] = h_in[kind, :, cut].astype(jnp.float32)
 
         def turn_h(low_bits, carry, column=column):
             for kind in range(2):
@@ -491,8 +491,8 @@
             pltpu.VMEM((span, channels), bf16),
             pltpu.VMEM((span, channels), bf16),
             pltpu.VMEM((2, span, channels), bf16),
-            pltpu.VMEM((channels * 2 * SUB, LANES), f32),
-            pltpu.VMEM((PER, span, LANES), f32),
+            pltpu.VMEM(((channels + 1) * 2 * SUB, LANES), f32),
+            pltpu.VMEM((PER, span + SUB, LANES), f32),
             pltpu.VMEM((n_seq, PER, 2 * SUB, LANES), bf16),
             pltpu.VMEM((n_seq, PER, 2 * SUB, LANES), bf16),
             pltpu.VMEM((n_seq, 2, PER, SUB, LANES), bf16),

time: 140 us -> 140 us (level)
  no operation moved by 1% of the time
where the time goes in v6:
time: 140 us
  Pallas kernels  139 us (99%)
    pallas_call x1, Pallas kernels, mixer(): pl.pallas_call(functools.partial(kernel, n_seq), out_shape=(pltpu.VMEM((2...  137 us

profile of v6, /device:TPU:7, one launch (start us, length us, event | category | flops | bytes accessed | tf_op | source)
XLA Modules:
  0.0 139.8 jit_solution(11433455447465360819)
XLA Ops:
  1.3 136.6 %shard_map.122 = (f32[2,2,1,512,384]{4,3,2,1,0:T(8,128)S(1)}, bf16[1,1024,384]{2,1,0:T(8,128)(2,1)S(1)}) custom-call(bf16[1,1024,384]{2,1,0:T(8,128)(2,1)} %z_hbm.1, bf16[1,1024,384]{2,1,0:T(8,128)(2,1)} %gate_hbm.1, bf16[1,1024,384]{2,1,0:T(8,128)(2,1)} %cot_hbm.1, bf16[2,2,1,1024,384]{4,3,2,1,0:T(8,128)(2,1)} %h_hbm.1, s32[1]{0:T(128)S(6)} %copy.13.limit_ref, ...), custom_call_target="tpu_custom_call" | custom-call | tf_op jit(solution)/shard_map/pallas_call | solution.py:479
  137.9 2.0 %shard_map.123 = (f32[2,2,1,512,384]{4,3,2,1,0:T(8,128)}, bf16[1,1024,384]{2,1,0:T(8,128)(2,1)}) custom-call(f32[2,2,1,512,384]{4,3,2,1,0:T(8,128)S(1)} %get-tuple-element.6.s_ref, bf16[1,1024,384]{2,1,0:T(8,128)(2,1)S(1)} %get-tuple-element.7.z_ref), custom_call_target="tpu_custom_call" | custom-call | tf_op jit(solution)/shard_map/pallas_call | solution.py:541
